TPU v7x, 512 devices: a whole 4x4x16 slice. The times are simulated.
512 devices in a mesh: space: 128 (over z, x, core), col: 4 (over y).
Axes of the slice: x: 4, y: 4, z: 16, core: 2. Of those that a mesh axis runs over, the one named last changes fastest.
Arguments:
- edge_embed: bfloat16 [16384, 512], P('space', 'col'), may hold values from -6 to 6
- atom_embed: bfloat16 [1024, 256], P('space'), may hold values from -6 to 6
- cotangent: bfloat16 [16384, 512], P('space', 'col'), may hold values from -6 to 6
- trip_basis: bfloat16 [524288, 64], P('space'), may hold values from -6 to 6
- weight_in: bfloat16 [512, 512], P(None, 'col'), may hold values from -0.21875 to 0.21875
- weight_atom: bfloat16 [256, 512], P(None, 'col'), may hold values from -0.21875 to 0.21875
- weight_basis: bfloat16 [64, 512], P(None, 'col'), may hold values from -0.125 to 0.125
- weight_out: bfloat16 [512, 512], P(None, 'col'), may hold values from -0.25 to 0.25
- atom_index: int32 [16384], P('space'), may hold values from 0 to 7
- trip_source: int32 [524288], P('space'), may hold values from 0 to 1151, as said below
- trip_target: int32 [524288], P('space'), may hold values from 0 to 127
- send_rows: int32 [128, 1024], P('space'), may hold values from 0 to 127
Outputs:
- grad_edge: bfloat16 [16384, 512], P('space', 'col')
- grad_atom: float32 [1024, 256], P('space')
- grad_w_in: float32 [512, 512], P(None, 'col')
- grad_w_atom: float32 [256, 512], P(None, 'col')
- grad_w_basis: float32 [64, 512], P(None, 'col')
- grad_w_out: float32 [512, 512], P(None, 'col')
Inputs may be any that keep to these rules, and one draw needn't show every extreme that they name: `trip_source`: index into the region's 128 edges followed by its 1024 boundary slots (slot j from region s at 128 + s * 8 + j). For each pair of regions only the first 1 to 8 slots are ever referenced; that count is 8 from both neighbouring regions (s = r - 1 and r + 1, modulo 128) and 0 from the region itself.
All inputs are finite; a program needn't handle non-finite values.
Results may differ from a plain program's by a relative error of at most 0.006.
Values may be sent and summed in bfloat16 or wider, within the bound.
No kernel may reach another device: no remote copies, remote signals or barrier semaphores. Data moves between devices by JAX's collectives and lax.ppermute only.
A program may use at most 64 MiB of HBM per device.

v0:
```python
import math

import jax
import jax.numpy as jnp
from jax import lax
from jax.sharding import PartitionSpec as P


def silu_slope(preact):
    sigmoid_pre = jax.nn.sigmoid(preact)
    return sigmoid_pre * (1.0 + preact * (1.0 - sigmoid_pre))


def body(
    edge_embed,
    atom_embed,
    cotangent,
    trip_basis,
    weight_in,
    weight_atom,
    weight_basis,
    weight_out,
    atom_index,
    trip_source,
    trip_target,
    send_rows,
):
    edge_rows = edge_embed.shape[0]
    atom_rows = atom_embed.shape[0]
    width_col = edge_embed.shape[1]
    basis_width = trip_basis.shape[1]
    trip_rows = trip_source.shape[0]
    blocks = edge_rows // 128
    per_block = trip_rows // blocks
    grad_scale = 1.0 / math.sqrt(edge_rows * lax.axis_size("space"))
    edge_full = lax.all_gather(edge_embed, "col", axis=1, tiled=True)
    atom_table = atom_index[:, None] == jnp.arange(atom_rows, dtype=jnp.int32)[None, :]
    atom_edge = jnp.dot(
        atom_table.astype(jnp.bfloat16), atom_embed, preferred_element_type=jnp.float32
    ).astype(jnp.bfloat16)
    preact = jnp.dot(edge_full, weight_in, preferred_element_type=jnp.float32) + jnp.dot(
        atom_edge, weight_atom, preferred_element_type=jnp.float32
    )
    active = jax.nn.silu(preact).astype(jnp.bfloat16)
    send_list = send_rows[0]
    incoming = lax.all_to_all(active[send_list], "space", split_axis=0, concat_axis=0, tiled=True)
    extended = jnp.concatenate([active, incoming], axis=0)
    partial_msg = jnp.einsum("ec,dc->ed", cotangent, weight_out, preferred_element_type=jnp.float32)
    grad_msg = lax.psum_scatter(partial_msg, "col", scatter_dimension=1, tiled=True)
    grad_msg = grad_msg.astype(jnp.bfloat16)
    source_blocks = trip_source.reshape(blocks, per_block)
    target_blocks = trip_target.reshape(blocks, per_block)
    basis_blocks = trip_basis.reshape(blocks, per_block, basis_width)
    grad_blocks = grad_msg.reshape(blocks, 128, width_col)
    lane_ids = jnp.arange(128, dtype=jnp.int32)

    def triplet_block(running, block_items):
        grad_ext, grad_bw = running
        source, target, basis_here, grad_here = block_items
        basis_val = jnp.dot(basis_here, weight_basis, preferred_element_type=jnp.float32)
        gathered = extended[source].astype(jnp.float32)
        select = (lane_ids[:, None] == target[None, :]).astype(jnp.bfloat16)
        product = (basis_val * gathered).astype(jnp.bfloat16)
        message_block = jnp.dot(select, product, preferred_element_type=jnp.float32).astype(
            jnp.bfloat16
        )
        spread = jnp.einsum("et,ec->tc", select, grad_here, preferred_element_type=jnp.float32)
        grad_basis = (spread * gathered).astype(jnp.bfloat16)
        grad_bw = grad_bw + jnp.einsum(
            "tb,tc->bc", basis_here, grad_basis, preferred_element_type=jnp.float32
        )
        grad_ext = grad_ext.at[source].add(spread * basis_val)
        return ((grad_ext, grad_bw), message_block)

    start = (
        jnp.zeros((extended.shape[0], width_col), jnp.float32),
        jnp.zeros((basis_width, width_col), jnp.float32),
    )
    (grad_ext, grad_bw), message = lax.scan(
        triplet_block, start, (source_blocks, target_blocks, basis_blocks, grad_blocks)
    )
    message = message.reshape(edge_rows, width_col)
    message_full = lax.all_gather(message, "col", axis=1, tiled=True)
    local_out = jnp.einsum("ed,ec->dc", message_full, cotangent, preferred_element_type=jnp.float32)
    returned = lax.all_to_all(
        grad_ext[edge_rows:], "space", split_axis=0, concat_axis=0, tiled=True
    )
    grad_act = grad_ext[:edge_rows].at[send_list].add(returned)
    grad_pre = (grad_act * silu_slope(preact)).astype(jnp.bfloat16)
    partial_edge = jnp.einsum("ec,dc->ed", grad_pre, weight_in, preferred_element_type=jnp.float32)
    grad_edge = lax.psum_scatter(partial_edge, "col", scatter_dimension=1, tiled=True).astype(
        jnp.bfloat16
    )
    partial_atom = jnp.einsum(
        "ec,ac->ea", grad_pre, weight_atom, preferred_element_type=jnp.float32
    )
    atom_part = jnp.einsum(
        "ea,eh->ah", atom_table.astype(jnp.float32), partial_atom, precision=lax.Precision.HIGHEST
    )
    grad_atom = lax.psum(atom_part, "col")
    local_in = jnp.einsum("ed,ec->dc", edge_full, grad_pre, preferred_element_type=jnp.float32)
    local_atom = jnp.einsum("eh,ec->hc", atom_edge, grad_pre, preferred_element_type=jnp.float32)
    sum_in, sum_atom, sum_basis, sum_out = lax.psum(
        (local_in, local_atom, grad_bw, local_out), "space"
    )
    return (
        grad_edge,
        grad_atom,
        sum_in * grad_scale,
        sum_atom * grad_scale,
        sum_basis * grad_scale,
        sum_out * grad_scale,
    )


def solution(mesh):
    placed = (
        P("space", "col"),
        P("space", None),
        P("space", "col"),
        P("space", None),
        P(None, "col"),
        P(None, "col"),
        P(None, "col"),
        P(None, "col"),
        P("space"),
        P("space"),
        P("space"),
        P("space", None),
    )
    return jax.shard_map(
        body,
        mesh=mesh,
        in_specs=placed,
        out_specs=(
            P("space", "col"),
            P("space", None),
            P(None, "col"),
            P(None, "col"),
            P(None, "col"),
            P(None, "col"),
        ),
        check_vma=False,
    )
```

profile of v0, /device:TPU:1, one launch (start us, length us, event | category | flops | bytes accessed | tf_op | source)
XLA Modules:
  0.0 704.3 jit_solution(14904201067668356553)
XLA Ops:
  7.2 1.9 fusion.18
  9.1 1.3 broadcast_clamp_fusion
  10.5 2.5 fusion.19
  13.0 29.8 %reduce-scatter.3.cloned.1.call-done = f32[128,128]{1,0:T(8,128)} async-done(((f32[128,512]{1,0:T(8,128)}), f32[128,128]{1,0:T(8,128)}) %reduce-scatter.3.cloned.1.call-update) | async-done | bytes 65552 | tf_op jit(solution)/shard_map/reduce_scatter | solution.py:49
  42.8 1.6 fusion.5
  44.4 23.0 %scatter_custom_fusion = f32[1152,128]{1,0:T(8,128)S(1)} fusion(s32[4096]{0:T(1024)S(1)} %get-tuple-element.57, f32[4096,128]{1,0:T(8,128)S(1)} %fusion.5, f32[4096,128]{1,0:T(8,128)} %fusion.19, f32[]{:T(128)} %constant.9.clone.1), kind=kCustom, calls=%fused_computation.8 | custom fusion | flops 1048576 | bytes 4784132 | tf_op jit(solution)/shard_map/while/body/eval_jaxpr/scatter-add | solution.py:72
  67.5 0.8 slice_bitcast_fusion
  68.3 19.3 %all-to-all-start = ((f32[128,8,128]{2,1,0:T(8,128)}), f32[128,8,128]{2,1,0:T(8,128)}, u32[]{:S(2)}, u32[]{:S(2)}) async-start(f32[128,8,128]{2,1,0:T(8,128)} %slice_bitcast_fusion), calls=%async_computation.1 | async-start | bytes 1048576 | tf_op jit(solution)/shard_map/all_to_all | solution.py:85
  87.6 9.6 %all_gather.6 = bf16[128,512]{1,0:T(8,128)(2,1)S(1)} all-gather(bf16[128,128]{1,0:T(8,128)(2,1)S(1)} %copy-done.6), channel_id=1, replica_groups=mesh['space'=128,'col'=4] {'col'}, dimensions={1}, use_global_device_ids=true | all-gather | bytes 163840 | tf_op jit(solution)/shard_map/all_gather | solution.py:36
  98.4 0.9 convolution_convert_fusion
  99.3 0.8 fusion.20
  100.7 17.3 %all-to-all-done = f32[128,8,128]{2,1,0:T(8,128)} async-done(((f32[128,8,128]{2,1,0:T(8,128)}), f32[128,8,128]{2,1,0:T(8,128)}, u32[]{:S(2)}, u32[]{:S(2)}) %all-to-all-start) | async-done | bytes 524320 | tf_op jit(solution)/shard_map/all_to_all | solution.py:85
  118.1 7.9 %scatter_custom_fusion.1 = f32[128,128]{1,0:T(8,128)} fusion(f32[128,128]{1,0:T(8,128)} %slice.12, s32[1024]{0:T(1024)} %bitcast.37, f32[128,8,128]{2,1,0:T(8,128)} %all-to-all-done), kind=kCustom, calls=%fused_computation.21 | custom fusion | flops 131072 | bytes 589824 | tf_op jit(solution)/shard_map/scatter-add | solution.py:88
  125.9 1.1 multiply_convert_fusion
  127.1 4.6 gather_fusion
  131.7 9.1 %all-to-all-start.1 = ((bf16[128,8,128]{2,1,0:T(8,128)(2,1)}), bf16[128,8,128]{2,1,0:T(8,128)(2,1)S(1)}, u32[]{:S(2)}, u32[]{:S(2)}) async-start(bf16[128,8,128]{2,1,0:T(8,128)(2,1)} %bitcast.5), calls=%async_computation.3 | async-start | bytes 524288 | tf_op jit(solution)/shard_map/all_to_all | solution.py:46
  140.8 0.9 fusion.21
  142.3 7.8 %psum.35 = f32[8,256]{1,0:T(8,128)} all-reduce(f32[8,256]{1,0:T(8,128)S(1)} %fusion.14), channel_id=1, replica_groups=mesh['space'=128,'col'=4] {'col'}, use_global_device_ids=true, to_apply=%region_4.5 | all-reduce | flops 2048 | bytes 16384 | tf_op jit(solution)/shard_map/psum | solution.py:100
  150.1 0.8 fusion.23
  150.9 0.9 convolution_bitcast_fusion
  151.8 18.8 %reduce-scatter.5.cloned.1.call-done = f32[128,128]{1,0:T(8,128)} async-done(((f32[128,512]{1,0:T(8,128)}), f32[128,128]{1,0:T(8,128)}) %reduce-scatter.5.cloned.1.call-update) | async-done | bytes 65552 | tf_op jit(solution)/shard_map/reduce_scatter | solution.py:91
  170.6 1.5 convert_element_type.38
  172.1 16.2 %gather_fusion.1 = bf16[4096,128]{1,0:T(8,128)(2,1)} fusion(bf16[1152,128]{1,0:T(8,128)(2,1)S(1)} %pad_maximum_fusion, s32[4096]{0:T(1024)} %get-tuple-element.56), kind=kCustom, calls=%fused_computation.1 | custom fusion | bytes 2113536 | tf_op jit(solution)/shard_map/while/body/eval_jaxpr/gather | solution.py:61
  188.3 2.5 fusion.6
  190.9 8.4 %all_gather.7 = bf16[128,512]{1,0:T(8,128)(2,1)S(1)} all-gather(bf16[128,128]{1,0:T(8,128)(2,1)S(1)} %fusion.6), channel_id=1, replica_groups=mesh['space'=128,'col'=4] {'col'}, dimensions={1}, use_global_device_ids=true | all-gather | bytes 163840 | tf_op jit(solution)/shard_map/all_gather | solution.py:83
  199.2 0.9 fusion.24
  200.2 1.6 convolution_bitcast_fusion.1
  201.8 491.9 %psum.38 = f32[64,128]{1,0:T(8,128)S(1)} all-reduce(f32[64,128]{1,0:T(8,128)S(1)} %convolution_bitcast_fusion.1), channel_id=1, replica_groups=mesh['space'=128,'col'=4] {'space'}, use_global_device_ids=true, to_apply=%region_7.8 | all-reduce | flops 8192 | bytes 65536 | tf_op jit(solution)/shard_map/psum | solution.py:103
  694.3 1.1 broadcast_multiply_fusion
  695.4 0.8 copy.22
  696.2 0.8 copy.23
  697.1 0.7 broadcast_multiply_fusion.2
  (35 shorter events, 3.1 us)
Async XLA Ops:
  7.2 3.3 copy-start
  7.2 35.7 %copy-start.4 = (s32[4096]{0:T(1024)S(1)}, s32[4096]{0:T(1024)}, u32[]{:S(2)}) copy-start(s32[4096]{0:T(1024)} %param.22) | copy-start | bytes 49156
  7.2 35.6 %reduce-scatter.3.cloned.1.call-start = ((), (), s32[]{:S(2)}) async-start(), calls=%async_computation.4 | async-start | bytes 327680 | tf_op jit(solution)/shard_map/reduce_scatter | solution.py:49
  67.5 20.1 %copy-start.6 = (bf16[128,128]{1,0:T(8,128)(2,1)S(1)}, bf16[128,128]{1,0:T(8,128)(2,1)}, u32[]{:S(2)}) copy-start(bf16[128,128]{1,0:T(8,128)(2,1)} %param.12) | copy-start | bytes 98308
  67.5 29.7 %copy-start.8 = (s32[1,1024]{1,0:T(1,128)S(1)}, s32[1,1024]{1,0:T(1,128)}, u32[]{:S(2)}) copy-start(s32[1,1024]{1,0:T(1,128)} %param.23) | copy-start | bytes 12292
  67.5 31.8 %copy-start.1 = (bf16[512,128]{1,0:T(8,128)(2,1)S(1)}, bf16[512,128]{1,0:T(8,128)(2,1)}, u32[]{:S(2)}) copy-start(bf16[512,128]{1,0:T(8,128)(2,1)} %param.16) | copy-start | bytes 393220
  68.3 49.7 %all-to-all-start = ((f32[128,8,128]{2,1,0:T(8,128)}), f32[128,8,128]{2,1,0:T(8,128)}, u32[]{:S(2)}, u32[]{:S(2)}) async-start(f32[128,8,128]{2,1,0:T(8,128)} %slice_bitcast_fusion), calls=%async_computation.1 | async-start | bytes 1048576 | tf_op jit(solution)/shard_map/all_to_all | solution.py:85
  97.2 0.6 copy-start.7
  125.9 15.9 %copy-start.5 = (bf16[256,128]{1,0:T(8,128)(2,1)S(1)}, bf16[256,128]{1,0:T(8,128)(2,1)}, u32[]{:S(2)}) copy-start(bf16[256,128]{1,0:T(8,128)(2,1)} %param.17) | copy-start | bytes 196612
  125.9 16.0 %copy-start.9 = (s32[128]{0:T(128)S(1)}, s32[128]{0:T(128)}, u32[]{:S(2)}) copy-start(s32[128]{0:T(128)} %param.20) | copy-start | bytes 1540
  131.7 40.4 %all-to-all-start.1 = ((bf16[128,8,128]{2,1,0:T(8,128)(2,1)}), bf16[128,8,128]{2,1,0:T(8,128)(2,1)S(1)}, u32[]{:S(2)}, u32[]{:S(2)}) async-start(bf16[128,8,128]{2,1,0:T(8,128)(2,1)} %bitcast.5), calls=%async_computation.3 | async-start | bytes 524288 | tf_op jit(solution)/shard_map/all_to_all | solution.py:46
  140.8 29.8 %reduce-scatter.5.cloned.1.call-start = ((), (), s32[]{:S(2)}) async-start(), calls=%async_computation.5 | async-start | bytes 327680 | tf_op jit(solution)/shard_map/reduce_scatter | solution.py:91
  141.7 552.5 %all-reduce.3.cloned.1.call-start = ((), (), s32[]{:S(2)}) async-start(), calls=%async_computation.6 | async-start | bytes 1310720 | tf_op jit(solution)/shard_map/psum | solution.py:103
  188.3 10.9 %copy-start.3 = (bf16[128,128]{1,0:T(8,128)(2,1)S(1)}, bf16[128,128]{1,0:T(8,128)(2,1)}, u32[]{:S(2)}) copy-start(bf16[128,128]{1,0:T(8,128)(2,1)} %param.14) | copy-start | bytes 98308
  694.3 2.8 copy-start.2
Sparse Core Ops, SparseCore 0:
  11.4 31.3 reduce-scatter.2
  145.2 25.3 reduce-scatter.4
  200.3 342.8 all-reduce.2
where the time goes:
time: 709 us; the launch traced here: 704 us
  blocking collectives  518 us (73%)
  waiting for transfers between devices  66 us (9%)
  other arithmetic  36.7 us (5%)
  starting transfers between devices  28.5 us (4%)
  local copies, waits for them, and re-layouts  24.6 us (3%)
  matrix products  16.9 us (2%)
  between operations  13.9 us (2%)
    psum x1, blocking collectives, body(): lax.psum((local_in, local_atom, grad_bw, local_out), 'space')  492 us
    reduce_scatter x1, waiting for transfers between devices, body(): lax.psum_scatter(partial_msg, 'col', scatter_dimension=1, tiled=True)  29.8 us
    scatter-add x1, other arithmetic, triplet_block(): grad_ext = grad_ext.at[source].add(spread * basis_val)  23 us
    all_to_all x1, starting transfers between devices, body(): lax.all_to_all(grad_ext[edge_rows:], 'space', split_axis=0, concat_axis=0...  19.3 us
    reduce_scatter x1, waiting for transfers between devices, body(): lax.psum_scatter(partial_edge, 'col', scatter_dimension=1, tiled=True)  18.8 us
    all_to_all x1, waiting for transfers between devices, body(): lax.all_to_all(grad_ext[edge_rows:], 'space', split_axis=0, concat_axis=0...  17.3 us
    gather x1, local copies, waits for them, and re-layouts, triplet_block(): gathered = extended[source].astype(jnp.float32)  16.2 us
  transfers between devices with their start and end apart: 5, of which 3 were waited for; matrix products, arithmetic and copies ran while one was open for 2% of the time, Pallas kernels for 0%

commit v1 on v0

v1 whole, which is shorter than its diff:
```python
import functools
import math

import jax
import jax.numpy as jnp
from jax import lax
from jax.experimental import pallas as pl
from jax.experimental.pallas import tpu as pltpu
from jax.sharding import PartitionSpec as P

F32 = jnp.float32
BF16 = jnp.bfloat16
VMEM = pl.BlockSpec(memory_space=pltpu.VMEM)
ROWS = 1408
STEP = 512


def call(kernel, outs, *args, scratch=(), flops=0):
    total = sum(math.prod(o.shape) * o.dtype.itemsize for o in outs)
    total += sum(a.size * a.dtype.itemsize for a in args)
    return pl.pallas_call(
        kernel,
        out_shape=list(outs),
        in_specs=[VMEM] * len(args),
        out_specs=[VMEM] * len(outs),
        scratch_shapes=list(scratch),
        compiler_params=pltpu.CompilerParams(vmem_limit_bytes=40 * 1024 * 1024),
        cost_estimate=pl.CostEstimate(flops=flops, bytes_accessed=total, transcendentals=0),
    )(*args)


def shape(*dims, dtype=F32):
    return jax.ShapeDtypeStruct(dims, dtype)


def dot(a, b, dims=((1,), (0,))):
    return lax.dot_general(a, b, (dims, ((), ())), preferred_element_type=F32)


def dot_nt(a, b):
    return dot(a, b, ((1,), (1,)))


def dot_tn(a, b):
    return dot(a, b, ((0,), (0,)))


def one_hot(mask):
    return jnp.where(mask, 1.0, 0.0).astype(BF16)


def iota(rows, lanes, axis):
    return lax.broadcasted_iota(jnp.int32, (rows, lanes), axis)


def block_of(ref, index):
    return ref[pl.ds(pl.multiple_of(index * 128, 128), 128), :]


def near(distance):
    return lax.axis_index("col") ^ distance


def bit_of(level):
    return lax.rem(lax.axis_index("space") // (1 << level), 2)


def sigmoid(value):
    return 1.0 / (1.0 + jnp.exp(-value))


def edge_kernel(
    edge_ref, atom_ref, win_ref, watom_ref, index_ref, send_ref,
    pre_ref, act_ref, out_ref, ae_ref,
):
    index = index_ref[...]
    at = one_hot(iota(8, 128, 0) == index)
    atom_edge = dot_tn(at, atom_ref[...]).astype(BF16)
    ae_ref[...] = atom_edge
    pre = dot(atom_edge, watom_ref[...])
    for c in range(4):
        pre = pre + dot(edge_ref[c], win_ref[c * 128 : (c + 1) * 128, :])
    pre_ref[...] = pre
    act = (pre * sigmoid(pre)).astype(BF16)
    act_ref[...] = act
    for i in range(8):
        pick = one_hot(iota(128, 128, 0) == send_ref[i : i + 1, :])
        out_ref[i * 128 : (i + 1) * 128, :] = dot_tn(pick, act).astype(BF16)


def scatter_kernel(
    cot_ref, wout_ref, basis_ref, wb_ref, source_ref, target_ref,
    gm_ref, own_ref, halo_ref, acc_ref,
):
    mine = pl.ds(pl.multiple_of(lax.axis_index("col") * 128, 128), 128)
    total = dot_nt(cot_ref[0], wout_ref[0, mine, :])
    for c in range(1, 4):
        total = total + dot_nt(cot_ref[c], wout_ref[c, mine, :])
    gm = total.astype(BF16)
    gm_ref[...] = gm
    wb = wb_ref[...]
    rows = acc_ref.shape[0]
    for c in range(source_ref.shape[0] * 128 // STEP):
        lines = range(c * STEP // 128, (c + 1) * STEP // 128)
        basis = basis_ref[:, c * STEP : (c + 1) * STEP]
        bv = dot_tn(basis, wb)
        sel = jnp.concatenate(
            [one_hot(iota(128, 128, 0) == target_ref[i : i + 1, :]) for i in lines], axis=1
        )
        spread = dot_tn(sel, gm)
        exact = spread * bv
        high = exact.astype(BF16)
        low = (exact - high.astype(F32)).astype(BF16)
        put = jnp.concatenate(
            [one_hot(iota(rows, 128, 0) == source_ref[i : i + 1, :]) for i in lines], axis=1
        )
        both = dot(put, jnp.concatenate([high, low], axis=1))
        part = both[:, :128] + both[:, 128:]
        if c == 0:
            acc_ref[...] = part
        else:
            acc_ref[...] += part
    own_ref[...] = acc_ref[:128, :]
    halo_ref[...] = acc_ref[128:, :].astype(BF16)


def gather_kernel(
    act_ref, in_ref, gm_ref, basis_ref, wb_ref, source_ref, target_ref,
    msg_ref, bw_ref, ext_ref,
):
    ext_ref[:128, :] = act_ref[...]
    ext_ref[128:, :] = in_ref[...]
    ext = ext_ref[...]
    gm = gm_ref[...]
    wb = wb_ref[...]
    rows = ext_ref.shape[0]
    msg = jnp.zeros((128, 128), F32)
    bw = jnp.zeros(bw_ref.shape, F32)
    for c in range(source_ref.shape[0] * 128 // STEP):
        lines = range(c * STEP // 128, (c + 1) * STEP // 128)
        basis = basis_ref[:, c * STEP : (c + 1) * STEP]
        bv = dot_tn(basis, wb)
        sel = jnp.concatenate(
            [one_hot(iota(128, 128, 0) == target_ref[i : i + 1, :]) for i in lines], axis=1
        )
        spread = dot_tn(sel, gm)
        cols = jnp.concatenate(
            [jnp.broadcast_to(source_ref[i : i + 1, :], (128, 128)).T for i in lines], axis=0
        )
        pick = jnp.concatenate(
            [one_hot(cols == iota(STEP, 128, 1) + 128 * k) for k in range(rows // 128)], axis=1
        )
        z = dot(pick, ext)
        msg = msg + dot(sel, (bv * z).astype(BF16))
        bw = bw + dot(basis, (spread * z).astype(BF16))
    msg_ref[...] = msg.astype(BF16)
    bw_ref[...] = bw


def weight_kernel(
    ret_ref, own_ref, pre_ref, send_ref, edge_ref, ae_ref, win_ref, watom_ref, index_ref,
    msg_ref, cot_ref, bw_ref,
    out_ref, keep_ref, col_send, col_keep, acc_ref,
):
    ga = own_ref[...]
    for i in range(8):
        put = one_hot(iota(128, 128, 0) == send_ref[i : i + 1, :])
        ga = ga + dot(put, ret_ref[i * 128 : (i + 1) * 128, :])
    pre = pre_ref[...]
    sig = sigmoid(pre)
    gp = (ga * (sig * (1.0 + pre * (1.0 - sig)))).astype(BF16)
    cot = cot_ref[...]
    for c in range(4):
        acc_ref[c * 128 : (c + 1) * 128, :] = dot_tn(edge_ref[c], gp)
        acc_ref[768 + c * 128 : 896 + c * 128, :] = dot_tn(msg_ref[c], cot)
    acc_ref[512:768, :] = dot_tn(ae_ref[...], gp)
    acc_ref[1280:1344, :] = bw_ref[...]
    acc_ref[1344:, :] = jnp.zeros((ROWS - 1344, 128), F32)
    half = ROWS // 2
    mine = pl.multiple_of(bit_of(0) * half, 16)
    other = pl.multiple_of(half - mine, 16)
    keep_ref[...] = acc_ref[pl.ds(mine, half), :]
    out_ref[...] = acc_ref[pl.ds(other, half), :].astype(BF16)
    at = one_hot(iota(8, 128, 0) == index_ref[...])
    total = dot(at, gp)
    high = total.astype(BF16)
    low = (total - high.astype(F32)).astype(BF16)
    atom = dot_nt(high, watom_ref[...]) + dot_nt(low, watom_ref[...])
    col_keep[:128, :] = dot_nt(gp, block_of(win_ref, near(0)))
    col_keep[128:256, :] = dot_nt(gp, block_of(win_ref, near(2)))
    col_send[:128, :] = dot_nt(gp, block_of(win_ref, near(1))).astype(BF16)
    col_send[128:256, :] = dot_nt(gp, block_of(win_ref, near(3))).astype(BF16)
    split_atom(jnp.concatenate([atom[:, :128], atom[:, 128:]], axis=0), col_keep, col_send, 256)


def split_atom(atom, keep_ref, send_ref, place):
    high = atom.astype(BF16)
    low = (atom - high.astype(F32)).astype(BF16)
    send_ref[place : place + 16, :] = high
    send_ref[place + 16 : place + 32, :] = low
    keep_ref[place : place + 16, :] = high.astype(F32) + low.astype(F32)


def atom_sum(keep_ref, got_ref, place):
    high = got_ref[place : place + 16, :].astype(F32)
    return keep_ref[place : place + 16, :] + (high + got_ref[place + 16 : place + 32, :].astype(F32))


def col_kernel(keep_ref, got_ref, send_ref, own_ref):
    own_ref[:128, :] = keep_ref[:128, :] + got_ref[:128, :].astype(F32)
    send_ref[:128, :] = (keep_ref[128:256, :] + got_ref[128:256, :].astype(F32)).astype(BF16)
    split_atom(atom_sum(keep_ref, got_ref, 256), own_ref, send_ref, 128)


def col_final_kernel(keep_ref, got_ref, edge_ref, atom_ref):
    edge_ref[...] = (keep_ref[:128, :] + got_ref[:128, :].astype(F32)).astype(BF16)
    atom = atom_sum(keep_ref, got_ref, 128)
    atom_ref[:, :128] = atom[:8, :]
    atom_ref[:, 128:] = atom[8:, :]


def halve_kernel(level, keep_ref, got_ref, after_ref, send_ref, own_ref):
    half = send_ref.shape[0]
    mine = pl.multiple_of(bit_of(level) * half, 16)
    other = pl.multiple_of(half - mine, 16)
    send_ref[...] = (
        keep_ref[pl.ds(other, half), :] + got_ref[pl.ds(other, half), :].astype(F32)
    ).astype(BF16)
    own_ref[...] = keep_ref[pl.ds(mine, half), :] + got_ref[pl.ds(mine, half), :].astype(F32)


def add_kernel(own_ref, got_ref, after_ref, out_ref):
    out_ref[...] = (own_ref[...] + got_ref[...].astype(F32)).astype(BF16)


def z_sum_kernel(all_ref, out_ref):
    total = all_ref[0].astype(F32)
    for i in range(1, all_ref.shape[0]):
        total = total + all_ref[i].astype(F32)
    out_ref[...] = total.astype(BF16)


def final_kernel(scale, all_ref, win_ref, watom_ref, wb_ref, wout_ref, acc_ref):
    rows = all_ref.shape[1]
    for g in range(8):
        place = ((g % 2) * 4 + (g // 2 % 2) * 2 + g // 4) * rows
        acc_ref[place : place + rows, :] = all_ref[g].astype(F32) * scale
    win_ref[...] = acc_ref[:512, :]
    watom_ref[...] = acc_ref[512:768, :]
    wout_ref[...] = acc_ref[768:1280, :]
    wb_ref[...] = acc_ref[1280:1344, :]


def col_swap(array, distance):
    return lax.ppermute(array, "col", [(i, i ^ distance) for i in range(4)])


def space_swap(array, distance, extent):
    return lax.ppermute(array, "space", [(i, i ^ distance) for i in range(extent)])


def body(
    edge_embed,
    atom_embed,
    cotangent,
    trip_basis,
    weight_in,
    weight_atom,
    weight_basis,
    weight_out,
    atom_index,
    trip_source,
    trip_target,
    send_rows,
):
    extent = lax.axis_size("space")
    grad_scale = 1.0 / math.sqrt(edge_embed.shape[0] * extent)
    half = dict(dtype=BF16)
    source = trip_source.reshape(-1, 128)
    target = trip_target.reshape(-1, 128)
    send = send_rows.reshape(8, 128)
    index = atom_index.reshape(1, 128)

    basis = trip_basis.T
    edge_all = lax.all_gather(edge_embed, "col")
    cot_all = lax.all_gather(cotangent, "col")
    wout_all = lax.all_gather(weight_out, "col")
    preact, active, outgoing, atom_edge = call(
        edge_kernel,
        [shape(128, 128), shape(128, 128, **half), shape(1024, 128, **half), shape(128, 256, **half)],
        edge_all, atom_embed, weight_in, weight_atom, index, send,
    )
    incoming = lax.all_to_all(
        outgoing.reshape(extent, 8, 128), "space", split_axis=0, concat_axis=0, tiled=True
    ).reshape(1024, 128)
    grad_msg, grad_own, grad_halo = call(
        scatter_kernel,
        [shape(128, 128, **half), shape(128, 128), shape(1024, 128, **half)],
        cot_all, wout_all, basis, weight_basis, source, target,
        scratch=[pltpu.VMEM((1152, 128), F32)],
        flops=2 * 4096 * 1152 * 128,
    )
    returned = lax.all_to_all(
        grad_halo.reshape(extent, 8, 128), "space", split_axis=0, concat_axis=0, tiled=True
    ).reshape(1024, 128)
    message, grad_bw = call(
        gather_kernel,
        [shape(128, 128, **half), shape(64, 128)],
        active, incoming, grad_msg, basis, weight_basis, source, target,
        scratch=[pltpu.VMEM((1152, 128), BF16)],
        flops=2 * 4096 * 1152 * 128,
    )
    msg_all = lax.all_gather(message, "col")
    out, keep, col_out, col_keep = call(
        weight_kernel,
        [
            shape(ROWS // 2, 128, **half), shape(ROWS // 2, 128),
            shape(288, 128, **half), shape(272, 128),
        ],
        returned, grad_own, preact, send, edge_all, atom_edge, weight_in, weight_atom, index,
        msg_all, cotangent, grad_bw,
        scratch=[pltpu.VMEM((ROWS, 128), F32)],
    )
    rows = ROWS // 2
    after = col_keep
    for level in (1, 2):
        rows //= 2
        got = space_swap(out, 1 << (level - 1), extent)
        out, keep = call(
            functools.partial(halve_kernel, level),
            [shape(rows, 128, **half), shape(rows, 128)],
            keep, got, after,
        )
        if level == 1:
            col_out, col_keep = call(
                col_kernel, [shape(160, 128, **half), shape(144, 128)], col_keep, col_swap(col_out, 1)
            )
            after = col_keep
    grad_edge, grad_atom = call(
        col_final_kernel, [shape(128, 128, **half), shape(8, 256)], col_keep, col_swap(col_out, 2)
    )
    (out,) = call(
        add_kernel, [shape(rows, 128, **half)], keep, space_swap(out, 4, extent), grad_atom
    )
    groups = [[z * 8 + g for z in range(extent // 8)] for g in range(8)]
    out = lax.all_gather(out, "space", axis_index_groups=groups)
    (out,) = call(z_sum_kernel, [shape(rows, 128, **half)], out)
    groups = [[z * 8 + g for g in range(8)] for z in range(extent // 8)]
    out = lax.all_gather(out, "space", axis_index_groups=groups)
    sum_in, sum_atom, sum_basis, sum_out = call(
        functools.partial(final_kernel, grad_scale),
        [shape(512, 128), shape(256, 128), shape(64, 128), shape(512, 128)],
        out,
        scratch=[pltpu.VMEM((ROWS, 128), F32)],
    )
    return grad_edge, grad_atom, sum_in, sum_atom, sum_basis, sum_out


def solution(mesh):
    placed = (
        P("space", "col"),
        P("space", None),
        P("space", "col"),
        P("space", None),
        P(None, "col"),
        P(None, "col"),
        P(None, "col"),
        P(None, "col"),
        P("space"),
        P("space"),
        P("space"),
        P("space", None),
    )
    return jax.shard_map(
        body,
        mesh=mesh,
        in_specs=placed,
        out_specs=(
            P("space", "col"),
            P("space", None),
            P(None, "col"),
            P(None, "col"),
            P(None, "col"),
            P(None, "col"),
        ),
        check_vma=False,
    )
```

time: 709 us -> 178 us (0.25)
  blocking collectives: 518 us -> 88.5 us
  waiting for transfers between devices: 66 us -> 11 us
  other arithmetic: 36.7 us -> 0 us
  starting transfers between devices: 28.5 us -> 60.3 us
  local copies, waits for them, and re-layouts: 24.6 us -> 2.25 us
  matrix products: 16.9 us -> 0 us
  Pallas kernels: 0 us -> 14.9 us
  between operations: 13.9 us -> 0.81 us
    psum x2 -> x0, blocking collectives: 500 us -> none  [the longest x1 492 us: body(): lax.psum((local_in, local_atom, grad_bw, local_out), 'space')]
    all_gather x2 -> x6, blocking collectives: 18 us -> 88.5 us  [the longest x2 46.9 us: body(): out = lax.all_gather(out, 'space', axis_index_groups=groups)]
    reduce_scatter x2 -> x0, waiting for transfers between devices: 48.6 us -> none  [the longest x1 29.8 us: body(): lax.psum_scatter(partial_msg, 'col', scatter_dimension=1, tiled=True)]
    scatter-add x2 -> x0, other arithmetic: 30.9 us -> none  [the longest x1 23 us: triplet_block(): grad_ext = grad_ext.at[source].add(spread * basis_val)]
    gather x2 -> x0, local copies, waits for them, and re-layouts: 20.9 us -> none  [the longest x1 16.2 us: triplet_block(): gathered = extended[source].astype(jnp.float32)]
    dot_general x14 -> x0, matrix products: 16.9 us -> none  [the longest x1 2.55 us: triplet_block(): jnp.dot(basis_here, weight_basis, preferred_element_type=jnp.float32)]
    ppermute x0 -> x5, starting transfers between devices: none -> 16.6 us  [the longest x3 11.2 us: space_swap(): lax.ppermute(array, 'space', [(i, i ^ distance) for i in range(extent)])]
    all_to_all x2, starting transfers between devices: 28.4 us -> 43.7 us  [the longest x1 22.6 us: body(): lax.all_to_all(outgoing.reshape(extent, 8, 128), 'space', split_axis=0, c...]
  transfers between devices with their start and end apart: 5 -> 7, of which waited for: 3 -> 4; matrix products, arithmetic and copies ran while one was open for 2% -> 0% of each run, Pallas kernels for 0% -> 7%
where the time goes in v1:
time: 178 us
  blocking collectives  88.5 us (50%)
  starting transfers between devices  60.3 us (34%)
  Pallas kernels  14.9 us (8%)
  waiting for transfers between devices  11 us (6%)
  local copies, waits for them, and re-layouts  2.25 us (1%)
    all_gather x2, blocking collectives, body(): out = lax.all_gather(out, 'space', axis_index_groups=groups)  46.9 us
    all_to_all x1, starting transfers between devices, body(): lax.all_to_all(outgoing.reshape(extent, 8, 128), 'space', split_axis=0, c...  22.6 us
    all_to_all x1, starting transfers between devices, body(): lax.all_to_all(grad_halo.reshape(extent, 8, 128), 'space', split_axis=0,...  21.1 us
    pallas_call x11, Pallas kernels, call(): pl.pallas_call(kernel, out_shape=list(outs), in_specs=[VMEM] * len(args),...  14.9 us
    ppermute x3, starting transfers between devices, space_swap(): lax.ppermute(array, 'space', [(i, i ^ distance) for i in range(extent)])  11.2 us
    all_gather x1, blocking collectives, body(): edge_all = lax.all_gather(edge_embed, 'col')  10.8 us
    all_gather x1, blocking collectives, body(): wout_all = lax.all_gather(weight_out, 'col')  10.6 us
    all_gather x1, blocking collectives, body(): cot_all = lax.all_gather(cotangent, 'col')  10.1 us
  transfers between devices with their start and end apart: 7, of which 4 were waited for; matrix products, arithmetic and copies ran while one was open for 0% of the time, Pallas kernels for 7%

profile of v1, /device:TPU:1, one launch (start us, length us, event | category | flops | bytes accessed | tf_op | source)
XLA Modules:
  0.0 177.7 jit_solution(6554203722673461392)
XLA Ops:
  0.7 10.8 %all-gather.2 = bf16[512,128]{1,0:T(8,128)(2,1)S(1)} all-gather(bf16[128,128]{1,0:T(8,128)(2,1)} %param.12), channel_id=4, replica_groups=mesh['space'=128,'col'=4] {'col'}, dimensions={0}, use_global_device_ids=true | all-gather | bytes 163840 | tf_op jit(solution)/shard_map/all_gather | solution.py:285
  11.5 0.7 copy-done.4
  12.1 0.8 copy-done.1
  13.0 1.3 shard_map.164
  14.3 22.6 %all-to-all-start.1 = ((bf16[128,8,128]{2,1,0:T(8,128)(2,1)}), bf16[128,8,128]{2,1,0:T(8,128)(2,1)S(1)}, u32[]{:S(2)}, u32[]{:S(2)}) async-start(bf16[128,8,128]{2,1,0:T(8,128)(2,1)} %bitcast.10), calls=%async_computation.1 | async-start | bytes 524288 | tf_op jit(solution)/shard_map/all_to_all | solution.py:293
  36.9 0.0 copy-start.8
  36.9 10.1 %all-gather = bf16[512,128]{1,0:T(8,128)(2,1)S(1)} all-gather(bf16[128,128]{1,0:T(8,128)(2,1)S(1)} %copy-done.3), channel_id=2, replica_groups=mesh['space'=128,'col'=4] {'col'}, dimensions={0}, use_global_device_ids=true | all-gather | bytes 163840 | tf_op jit(solution)/shard_map/all_gather | solution.py:286
  47.1 0.0 copy-start.11
  47.1 10.6 %all-gather.1 = bf16[2048,128]{1,0:T(8,128)(2,1)S(1)} all-gather(bf16[512,128]{1,0:T(8,128)(2,1)S(1)} %copy-done.12), channel_id=3, replica_groups=mesh['space'=128,'col'=4] {'col'}, dimensions={0}, use_global_device_ids=true | all-gather | bytes 655360 | tf_op jit(solution)/shard_map/all_gather | solution.py:287
  57.7 4.6 %shard_map.163 = (bf16[128,128]{1,0:T(8,128)(2,1)S(1)}, f32[128,128]{1,0:T(8,128)S(1)}, bf16[1024,128]{1,0:T(8,128)(2,1)}) custom-call(bf16[4,128,128]{2,1,0:T(8,128)(2,1)S(1)} %bitcast.23, bf16[4,512,128]{2,1,0:T(8,128)(2,1)S(1)} %bitcast.21, bf16[64,4096]{1,0:T(8,128)(2,1)S(1)} %bitcast.28, bf16[64,128]{1,0:T(8,128)(2,1)S(1)} %copy-done.9, ...), custom_call_target="tpu_custom_call" | custom-call | flops 1207959552 | bytes 1589248 | tf_op jit(solution)/shard_map/pallas_call | solution.py:21
  62.3 0.0 all-to-all-done.1
  62.3 21.1 %all-to-all-start = ((bf16[128,8,128]{2,1,0:T(8,128)(2,1)}), bf16[128,8,128]{2,1,0:T(8,128)(2,1)S(1)}, u32[]{:S(2)}, u32[]{:S(2)}) async-start(bf16[128,8,128]{2,1,0:T(8,128)(2,1)} %bitcast.5), calls=%async_computation | async-start | bytes 524288 | tf_op jit(solution)/shard_map/all_to_all | solution.py:303
  83.4 6.4 %shard_map.165 = (bf16[128,128]{1,0:T(8,128)(2,1)S(1)}, f32[64,128]{1,0:T(8,128)S(1)}) custom-call(bf16[128,128]{1,0:T(8,128)(2,1)S(1)} %get-tuple-element.35.act_ref, bf16[1024,128]{1,0:T(8,128)(2,1)S(1)} %bitcast.22, bf16[128,128]{1,0:T(8,128)(2,1)S(1)} %get-tuple-element.37.gm_ref, bf16[64,4096]{1,0:T(8,128)(2,1)S(1)} %bitcast.29, ...), custom_call_target="tpu_custom_call" | custom-call | flops 1207959552 | bytes 966656 | tf_op jit(solution)/shard_map/pallas_call | solution.py:21
  89.8 0.0 copy-start.2
  89.8 10.1 %all-gather.3 = bf16[512,128]{1,0:T(8,128)(2,1)S(1)} all-gather(bf16[128,128]{1,0:T(8,128)(2,1)S(1)} %get-tuple-element.38), channel_id=5, replica_groups=mesh['space'=128,'col'=4] {'col'}, dimensions={0}, use_global_device_ids=true | all-gather | bytes 163840 | tf_op jit(solution)/shard_map/all_gather | solution.py:313
  100.0 4.0 %all-to-all-done = bf16[128,8,128]{2,1,0:T(8,128)(2,1)S(1)} async-done(((bf16[128,8,128]{2,1,0:T(8,128)(2,1)}), bf16[128,8,128]{2,1,0:T(8,128)(2,1)S(1)}, u32[]{:S(2)}, u32[]{:S(2)}) %all-to-all-start) | async-done | bytes 262176 | tf_op jit(solution)/shard_map/all_to_all | solution.py:303
  103.9 0.8 shard_map.166
  104.8 2.4 %collective-permute-start.2 = (bf16[704,128]{1,0:T(8,128)(2,1)S(1)}, bf16[704,128]{1,0:T(8,128)(2,1)S(1)}, u32[]{:S(2)}, u32[]{:S(2)}) collective-permute-start(bf16[704,128]{1,0:T(8,128)(2,1)S(1)} %get-tuple-element.47), channel_id=1, source_target_pairs={{0,4},{4,0},{8,12},{12,8},{16,20},{20,16},{24,28},{28,24},{32,36},... | collective-permute-start | bytes 540680 | tf_op jit(solution)/shard_map/ppermute | solution.py:259
  107.1 1.0 collective-permute-done.2.got_ref
  108.2 4.2 %collective-permute-start.3 = (bf16[352,128]{1,0:T(8,128)(2,1)S(1)}, bf16[352,128]{1,0:T(8,128)(2,1)S(1)}, u32[]{:S(2)}, u32[]{:S(2)}) collective-permute-start(bf16[352,128]{1,0:T(8,128)(2,1)S(1)} %get-tuple-element.49), channel_id=1, source_target_pairs={{0,8},{4,12},{8,0},{12,4},{16,24},{20,28},{24,16},{28,20},{32,40},... | collective-permute-start | bytes 270344 | tf_op jit(solution)/shard_map/ppermute | solution.py:259
  112.4 2.2 %collective-permute-start = (bf16[288,128]{1,0:T(8,128)(2,1)S(1)}, bf16[288,128]{1,0:T(8,128)(2,1)S(1)}, u32[]{:S(2)}, u32[]{:S(2)}) collective-permute-start(bf16[288,128]{1,0:T(8,128)(2,1)S(1)} %get-tuple-element.41), channel_id=1, source_target_pairs={{0,1},{1,0},{2,3},{3,2},{4,5},{5,4},{6,7},{7,6},{8,9},{9,8},{10,11... | collective-permute-start | bytes 221192 | tf_op jit(solution)/shard_map/ppermute | solution.py:255
  114.6 2.9 %collective-permute-done.got_ref = bf16[288,128]{1,0:T(8,128)(2,1)S(1)} collective-permute-done((bf16[288,128]{1,0:T(8,128)(2,1)S(1)}, bf16[288,128]{1,0:T(8,128)(2,1)S(1)}, u32[]{:S(2)}, u32[]{:S(2)}) %collective-permute-start) | collective-permute-done | bytes 73760 | tf_op jit(solution)/shard_map/ppermute | solution.py:255
  117.5 0.0 collective-permute-done.3.got_ref
  117.6 4.7 %collective-permute-start.4 = (bf16[176,128]{1,0:T(8,128)(2,1)S(1)}, bf16[176,128]{1,0:T(8,128)(2,1)S(1)}, u32[]{:S(2)}, u32[]{:S(2)}) collective-permute-start(bf16[176,128]{1,0:T(8,128)(2,1)S(1)} %get-tuple-element.51), channel_id=1, source_target_pairs={{0,16},{4,20},{8,24},{12,28},{16,0},{20,4},{24,8},{28,12},{32,48},... | collective-permute-start | bytes 135176 | tf_op jit(solution)/shard_map/ppermute | solution.py:259
  122.3 3.2 %collective-permute-start.1 = (bf16[160,128]{1,0:T(8,128)(2,1)S(1)}, bf16[160,128]{1,0:T(8,128)(2,1)S(1)}, u32[]{:S(2)}, u32[]{:S(2)}) collective-permute-start(bf16[160,128]{1,0:T(8,128)(2,1)S(1)} %get-tuple-element.43), channel_id=1, source_target_pairs={{0,2},{1,3},{2,0},{3,1},{4,6},{5,7},{6,4},{7,5},{8,10},{9,11},{10,... | collective-permute-start | bytes 122888 | tf_op jit(solution)/shard_map/ppermute | solution.py:255
  125.4 3.1 %collective-permute-done.1.got_ref = bf16[160,128]{1,0:T(8,128)(2,1)S(1)} collective-permute-done((bf16[160,128]{1,0:T(8,128)(2,1)S(1)}, bf16[160,128]{1,0:T(8,128)(2,1)S(1)}, u32[]{:S(2)}, u32[]{:S(2)}) %collective-permute-start.1) | collective-permute-done | bytes 40992 | tf_op jit(solution)/shard_map/ppermute | solution.py:255
  128.5 0.6 shard_map.168
  129.1 0.7 copy-done.5
  129.8 23.8 %all-gather.4 = bf16[2816,128]{1,0:T(8,128)(2,1)S(1)} all-gather(bf16[176,128]{1,0:T(8,128)(2,1)S(1)} %shard_map.171), channel_id=6, replica_groups={{0,32,64,96,128,160,192,224,256,288,320,352,384,416,448,480},{4,36,68,1..., dimensions={0}, use_global_device_ids=true | all-gather | bytes 765952 | tf_op jit(solution)/shard_map/all_gather | solution.py:346
  153.7 0.1 shard_map.172
  153.8 23.0 %all-gather.5 = bf16[1408,128]{1,0:T(8,128)(2,1)S(1)} all-gather(bf16[176,128]{1,0:T(8,128)(2,1)S(1)} %shard_map.172), channel_id=7, replica_groups={{0,4,8,12,16,20,24,28},{32,36,40,44,48,52,56,60},{64,68,72,76,80,84,88,..., dimensions={0}, use_global_device_ids=true | all-gather | bytes 405504 | tf_op jit(solution)/shard_map/all_gather | solution.py:349
  176.8 0.9 shard_map.173
  (25 shorter events, 0.2 us)
Async XLA Ops:
  0.6 10.8 %copy-start = (bf16[512,128]{1,0:T(8,128)(2,1)S(1)}, bf16[512,128]{1,0:T(8,128)(2,1)}, u32[]{:S(2)}) copy-start(bf16[512,128]{1,0:T(8,128)(2,1)} %win_ref.3) | copy-start | bytes 393220
  0.6 10.8 %copy-start.6 = (bf16[8,256]{1,0:T(8,128)(2,1)S(1)}, bf16[8,256]{1,0:T(8,128)(2,1)}, u32[]{:S(2)}) copy-start(bf16[8,256]{1,0:T(8,128)(2,1)} %atom_ref.1) | copy-start | bytes 12292
  11.5 0.7 copy-start.4
  11.5 0.7 copy-start.7
  12.1 0.8 copy-start.1
  14.3 22.6 %copy-start.3 = (bf16[128,128]{1,0:T(8,128)(2,1)S(1)}, bf16[128,128]{1,0:T(8,128)(2,1)}, u32[]{:S(2)}) copy-start(bf16[128,128]{1,0:T(8,128)(2,1)} %cot_ref.1) | copy-start | bytes 98308
  14.3 32.7 %copy-start.12 = (bf16[512,128]{1,0:T(8,128)(2,1)S(1)}, bf16[512,128]{1,0:T(8,128)(2,1)}, u32[]{:S(2)}) copy-start(bf16[512,128]{1,0:T(8,128)(2,1)} %param.19) | copy-start | bytes 393220
  14.3 48.0 %all-to-all-start.1 = ((bf16[128,8,128]{2,1,0:T(8,128)(2,1)}), bf16[128,8,128]{2,1,0:T(8,128)(2,1)S(1)}, u32[]{:S(2)}, u32[]{:S(2)}) async-start(bf16[128,8,128]{2,1,0:T(8,128)(2,1)} %bitcast.10), calls=%async_computation.1 | async-start | bytes 524288 | tf_op jit(solution)/shard_map/all_to_all | solution.py:293
  36.9 20.8 %copy-start.8 = (bf16[4096,64]{0,1:T(8,128)(2,1)S(1)}, bf16[4096,64]{0,1:T(8,128)(2,1)}, u32[]{:S(2)}) copy-start(bf16[4096,64]{0,1:T(8,128)(2,1)} %param.15) | copy-start | bytes 1572868
  47.1 10.6 %copy-start.9 = (bf16[64,128]{1,0:T(8,128)(2,1)S(1)}, bf16[64,128]{1,0:T(8,128)(2,1)}, u32[]{:S(2)}) copy-start(bf16[64,128]{1,0:T(8,128)(2,1)} %wb_ref.3) | copy-start | bytes 49156
  47.1 10.6 %copy-start.10 = (s32[4096]{0:T(1024)S(1)}, s32[4096]{0:T(1024)}, u32[]{:S(2)}) copy-start(s32[4096]{0:T(1024)} %param.21) | copy-start | bytes 49156
  47.1 10.6 %copy-start.11 = (s32[4096]{0:T(1024)S(1)}, s32[4096]{0:T(1024)}, u32[]{:S(2)}) copy-start(s32[4096]{0:T(1024)} %param.22) | copy-start | bytes 49156
  62.3 41.6 %all-to-all-start = ((bf16[128,8,128]{2,1,0:T(8,128)(2,1)}), bf16[128,8,128]{2,1,0:T(8,128)(2,1)S(1)}, u32[]{:S(2)}, u32[]{:S(2)}) async-start(bf16[128,8,128]{2,1,0:T(8,128)(2,1)} %bitcast.5), calls=%async_computation | async-start | bytes 524288 | tf_op jit(solution)/shard_map/all_to_all | solution.py:303
  89.8 14.1 %copy-start.2 = (bf16[256,128]{1,0:T(8,128)(2,1)S(1)}, bf16[256,128]{1,0:T(8,128)(2,1)}, u32[]{:S(2)}) copy-start(bf16[256,128]{1,0:T(8,128)(2,1)} %watom_ref.3) | copy-start | bytes 196612
  104.8 3.4 %collective-permute-start.2 = (bf16[704,128]{1,0:T(8,128)(2,1)S(1)}, bf16[704,128]{1,0:T(8,128)(2,1)S(1)}, u32[]{:S(2)}, u32[]{:S(2)}) collective-permute-start(bf16[704,128]{1,0:T(8,128)(2,1)S(1)} %get-tuple-element.47), channel_id=1, source_target_pairs={{0,4},{4,0},{8,12},{12,8},{16,20},{20,16},{24,28},{28,24},{32,36},... | collective-permute-start | bytes 540680 | tf_op jit(solution)/shard_map/ppermute | solution.py:259
  108.2 9.3 %collective-permute-start.3 = (bf16[352,128]{1,0:T(8,128)(2,1)S(1)}, bf16[352,128]{1,0:T(8,128)(2,1)S(1)}, u32[]{:S(2)}, u32[]{:S(2)}) collective-permute-start(bf16[352,128]{1,0:T(8,128)(2,1)S(1)} %get-tuple-element.49), channel_id=1, source_target_pairs={{0,8},{4,12},{8,0},{12,4},{16,24},{20,28},{24,16},{28,20},{32,40},... | collective-permute-start | bytes 270344 | tf_op jit(solution)/shard_map/ppermute | solution.py:259
  112.4 5.1 %collective-permute-start = (bf16[288,128]{1,0:T(8,128)(2,1)S(1)}, bf16[288,128]{1,0:T(8,128)(2,1)S(1)}, u32[]{:S(2)}, u32[]{:S(2)}) collective-permute-start(bf16[288,128]{1,0:T(8,128)(2,1)S(1)} %get-tuple-element.41), channel_id=1, source_target_pairs={{0,1},{1,0},{2,3},{3,2},{4,5},{5,4},{6,7},{7,6},{8,9},{9,8},{10,11... | collective-permute-start | bytes 221192 | tf_op jit(solution)/shard_map/ppermute | solution.py:255
  117.6 11.6 %collective-permute-start.4 = (bf16[176,128]{1,0:T(8,128)(2,1)S(1)}, bf16[176,128]{1,0:T(8,128)(2,1)S(1)}, u32[]{:S(2)}, u32[]{:S(2)}) collective-permute-start(bf16[176,128]{1,0:T(8,128)(2,1)S(1)} %get-tuple-element.51), channel_id=1, source_target_pairs={{0,16},{4,20},{8,24},{12,28},{16,0},{20,4},{24,8},{28,12},{32,48},... | collective-permute-start | bytes 135176 | tf_op jit(solution)/shard_map/ppermute | solution.py:259
  122.3 6.3 %collective-permute-start.1 = (bf16[160,128]{1,0:T(8,128)(2,1)S(1)}, bf16[160,128]{1,0:T(8,128)(2,1)S(1)}, u32[]{:S(2)}, u32[]{:S(2)}) collective-permute-start(bf16[160,128]{1,0:T(8,128)(2,1)S(1)} %get-tuple-element.43), channel_id=1, source_target_pairs={{0,2},{1,3},{2,0},{3,1},{4,6},{5,7},{6,4},{7,5},{8,10},{9,11},{10,... | collective-permute-start | bytes 122888 | tf_op jit(solution)/shard_map/ppermute | solution.py:255
  129.1 0.7 copy-start.5

commit v2 on v1

--- a/solution.py
+++ b/solution.py
@@ -88,14 +88,19 @@
         out_ref[i * 128 : (i + 1) * 128, :] = dot_tn(pick, act).astype(BF16)
 
 
+def pack_kernel(cot_ref, wout_ref, after_ref, out_ref):
+    out_ref[:128, :] = cot_ref[...]
+    out_ref[128:, :] = wout_ref[...]
+
+
 def scatter_kernel(
-    cot_ref, wout_ref, basis_ref, wb_ref, source_ref, target_ref,
+    gather_ref, basis_ref, wb_ref, source_ref, target_ref,
     gm_ref, own_ref, halo_ref, acc_ref,
 ):
-    mine = pl.ds(pl.multiple_of(lax.axis_index("col") * 128, 128), 128)
-    total = dot_nt(cot_ref[0], wout_ref[0, mine, :])
+    mine = pl.ds(pl.multiple_of(lax.axis_index("col") * 128 + 128, 128), 128)
+    total = dot_nt(gather_ref[0, :128, :], gather_ref[0, mine, :])
     for c in range(1, 4):
-        total = total + dot_nt(cot_ref[c], wout_ref[c, mine, :])
+        total = total + dot_nt(gather_ref[c, :128, :], gather_ref[c, mine, :])
     gm = total.astype(BF16)
     gm_ref[...] = gm
     wb = wb_ref[...]
@@ -160,7 +165,7 @@
 def weight_kernel(
     ret_ref, own_ref, pre_ref, send_ref, edge_ref, ae_ref, win_ref, watom_ref, index_ref,
     msg_ref, cot_ref, bw_ref,
-    out_ref, keep_ref, col_send, col_keep, acc_ref,
+    out_ref, keep_ref, edge_own, atom_own, col1, col2, col3, acc_ref,
 ):
     ga = own_ref[...]
     for i in range(8):
@@ -186,35 +191,24 @@
     high = total.astype(BF16)
     low = (total - high.astype(F32)).astype(BF16)
     atom = dot_nt(high, watom_ref[...]) + dot_nt(low, watom_ref[...])
-    col_keep[:128, :] = dot_nt(gp, block_of(win_ref, near(0)))
-    col_keep[128:256, :] = dot_nt(gp, block_of(win_ref, near(2)))
-    col_send[:128, :] = dot_nt(gp, block_of(win_ref, near(1))).astype(BF16)
-    col_send[128:256, :] = dot_nt(gp, block_of(win_ref, near(3))).astype(BF16)
-    split_atom(jnp.concatenate([atom[:, :128], atom[:, 128:]], axis=0), col_keep, col_send, 256)
-
-
-def split_atom(atom, keep_ref, send_ref, place):
+    edge_own[...] = dot_nt(gp, block_of(win_ref, near(0)))
+    atom = jnp.concatenate([atom[:, :128], atom[:, 128:]], axis=0)
     high = atom.astype(BF16)
     low = (atom - high.astype(F32)).astype(BF16)
-    send_ref[place : place + 16, :] = high
-    send_ref[place + 16 : place + 32, :] = low
-    keep_ref[place : place + 16, :] = high.astype(F32) + low.astype(F32)
-
-
-def atom_sum(keep_ref, got_ref, place):
-    high = got_ref[place : place + 16, :].astype(F32)
-    return keep_ref[place : place + 16, :] + (high + got_ref[place + 16 : place + 32, :].astype(F32))
-
-
-def col_kernel(keep_ref, got_ref, send_ref, own_ref):
-    own_ref[:128, :] = keep_ref[:128, :] + got_ref[:128, :].astype(F32)
-    send_ref[:128, :] = (keep_ref[128:256, :] + got_ref[128:256, :].astype(F32)).astype(BF16)
-    split_atom(atom_sum(keep_ref, got_ref, 256), own_ref, send_ref, 128)
-
-
-def col_final_kernel(keep_ref, got_ref, edge_ref, atom_ref):
-    edge_ref[...] = (keep_ref[:128, :] + got_ref[:128, :].astype(F32)).astype(BF16)
-    atom = atom_sum(keep_ref, got_ref, 128)
+    atom_own[...] = high.astype(F32) + low.astype(F32)
+    for d, ref in ((1, col1), (2, col2), (3, col3)):
+        ref[:128, :] = dot_nt(gp, block_of(win_ref, near(d))).astype(BF16)
+        ref[128:144, :] = high
+        ref[144:, :] = low
+
+
+def col_final_kernel(edge_own, atom_own, got1, got2, got3, edge_ref, atom_ref):
+    edge = edge_own[...]
+    atom = atom_own[...]
+    for got in (got1, got2, got3):
+        edge = edge + got[:128, :].astype(F32)
+        atom = atom + (got[128:144, :].astype(F32) + got[144:, :].astype(F32))
+    edge_ref[...] = edge.astype(BF16)
     atom_ref[:, :128] = atom[:8, :]
     atom_ref[:, 128:] = atom[8:, :]
 
@@ -229,7 +223,7 @@
     own_ref[...] = keep_ref[pl.ds(mine, half), :] + got_ref[pl.ds(mine, half), :].astype(F32)
 
 
-def add_kernel(own_ref, got_ref, after_ref, out_ref):
+def add_kernel(own_ref, got_ref, after2, after3, out_ref):
     out_ref[...] = (own_ref[...] + got_ref[...].astype(F32)).astype(BF16)
 
 
@@ -283,8 +277,6 @@
 
     basis = trip_basis.T
     edge_all = lax.all_gather(edge_embed, "col")
-    cot_all = lax.all_gather(cotangent, "col")
-    wout_all = lax.all_gather(weight_out, "col")
     preact, active, outgoing, atom_edge = call(
         edge_kernel,
         [shape(128, 128), shape(128, 128, **half), shape(1024, 128, **half), shape(128, 256, **half)],
@@ -293,10 +285,12 @@
     incoming = lax.all_to_all(
         outgoing.reshape(extent, 8, 128), "space", split_axis=0, concat_axis=0, tiled=True
     ).reshape(1024, 128)
+    (cot_wout,) = call(pack_kernel, [shape(640, 128, **half)], cotangent, weight_out, active)
+    cot_wout = lax.all_gather(cot_wout, "col")
     grad_msg, grad_own, grad_halo = call(
         scatter_kernel,
         [shape(128, 128, **half), shape(128, 128), shape(1024, 128, **half)],
-        cot_all, wout_all, basis, weight_basis, source, target,
+        cot_wout, basis, weight_basis, source, target,
         scratch=[pltpu.VMEM((1152, 128), F32)],
         flops=2 * 4096 * 1152 * 128,
     )
@@ -311,19 +305,19 @@
         flops=2 * 4096 * 1152 * 128,
     )
     msg_all = lax.all_gather(message, "col")
-    out, keep, col_out, col_keep = call(
+    out, keep, edge_own, atom_own, col1, col2, col3 = call(
         weight_kernel,
         [
-            shape(ROWS // 2, 128, **half), shape(ROWS // 2, 128),
-            shape(288, 128, **half), shape(272, 128),
+            shape(ROWS // 2, 128, **half), shape(ROWS // 2, 128), shape(128, 128), shape(16, 128),
+            shape(160, 128, **half), shape(160, 128, **half), shape(160, 128, **half),
         ],
         returned, grad_own, preact, send, edge_all, atom_edge, weight_in, weight_atom, index,
         msg_all, cotangent, grad_bw,
         scratch=[pltpu.VMEM((ROWS, 128), F32)],
     )
     rows = ROWS // 2
-    after = col_keep
-    for level in (1, 2):
+    got1, got2, got3 = (col_swap(part, d) for d, part in ((1, col1), (2, col2), (3, col3)))
+    for level, after in ((1, edge_own), (2, got1)):
         rows //= 2
         got = space_swap(out, 1 << (level - 1), extent)
         out, keep = call(
@@ -331,21 +325,20 @@
             [shape(rows, 128, **half), shape(rows, 128)],
             keep, got, after,
         )
-        if level == 1:
-            col_out, col_keep = call(
-                col_kernel, [shape(160, 128, **half), shape(144, 128)], col_keep, col_swap(col_out, 1)
-            )
-            after = col_keep
+    (out,) = call(
+        add_kernel, [shape(rows, 128, **half)], keep, space_swap(out, 4, extent), got2, got3
+    )
     grad_edge, grad_atom = call(
-        col_final_kernel, [shape(128, 128, **half), shape(8, 256)], col_keep, col_swap(col_out, 2)
-    )
-    (out,) = call(
-        add_kernel, [shape(rows, 128, **half)], keep, space_swap(out, 4, extent), grad_atom
-    )
-    groups = [[z * 8 + g for z in range(extent // 8)] for g in range(8)]
+        col_final_kernel, [shape(128, 128, **half), shape(8, 256)],
+        edge_own, atom_own, got1, got2, got3,
+    )
+    depth = extent // 8
+    groups = [
+        [(z if g % 2 == 0 else depth - 1 - z) * 8 + g for z in range(depth)] for g in range(8)
+    ]
     out = lax.all_gather(out, "space", axis_index_groups=groups)
     (out,) = call(z_sum_kernel, [shape(rows, 128, **half)], out)
-    groups = [[z * 8 + g for g in range(8)] for z in range(extent // 8)]
+    groups = [[z * 8 + g for g in range(8)] for z in range(depth)]
     out = lax.all_gather(out, "space", axis_index_groups=groups)
     sum_in, sum_atom, sum_basis, sum_out = call(
         functools.partial(final_kernel, grad_scale),

time: 178 us -> 169 us (0.949)
  blocking collectives: 88.5 us -> 79.8 us
  starting transfers between devices: 60.3 us -> 58.3 us
    all_gather x2 -> x1, blocking collectives: 20.7 us -> 12.1 us  [body(): cot_wout = lax.all_gather(cot_wout, 'col')]
    all_to_all x1, starting transfers between devices: 21.1 us -> 13.6 us  [body(): lax.all_to_all(grad_halo.reshape(extent, 8, 128), 'space', split_axis=0,...]
    ppermute x2 -> x3, starting transfers between devices: 5.38 us -> 10.9 us  [col_swap(): return lax.ppermute(array, 'col', [(i, i ^ distance) for i in range(4)])]
    all_to_all x1, waiting for transfers between devices: 0.01 us -> 3.74 us  [body(): lax.all_to_all(outgoing.reshape(extent, 8, 128), 'space', split_axis=0, c...]
    ppermute x2 -> x3, waiting for transfers between devices: 5.95 us -> 4.01 us  [col_swap(): return lax.ppermute(array, 'col', [(i, i ^ distance) for i in range(4)])]
  transfers between devices with their start and end apart: 7 -> 8, of which waited for: 4 -> 5; matrix products, arithmetic and copies ran while one was open for 0% -> 0% of each run, Pallas kernels for 7% -> 7%
where the time goes in v2:
time: 169 us; the launch traced here: 168 us
  blocking collectives  79.8 us (47%)
  starting transfers between devices  58.3 us (34%)
  Pallas kernels  14.8 us (9%)
  waiting for transfers between devices  12.7 us (8%)
    all_gather x2, blocking collectives, body(): out = lax.all_gather(out, 'space', axis_index_groups=groups)  46.8 us
    all_to_all x1, starting transfers between devices, body(): lax.all_to_all(outgoing.reshape(extent, 8, 128), 'space', split_axis=0, c...  22.6 us
    pallas_call x11, Pallas kernels, call(): pl.pallas_call(kernel, out_shape=list(outs), in_specs=[VMEM] * len(args),...  14.8 us
    all_to_all x1, starting transfers between devices, body(): lax.all_to_all(grad_halo.reshape(extent, 8, 128), 'space', split_axis=0,...  13.6 us
    all_gather x1, blocking collectives, body(): cot_wout = lax.all_gather(cot_wout, 'col')  12.1 us
    ppermute x3, starting transfers between devices, space_swap(): lax.ppermute(array, 'space', [(i, i ^ distance) for i in range(extent)])  11.2 us
    ppermute x3, starting transfers between devices, col_swap(): return lax.ppermute(array, 'col', [(i, i ^ distance) for i in range(4)])  10.9 us
    all_gather x1, blocking collectives, body(): edge_all = lax.all_gather(edge_embed, 'col')  10.8 us
  transfers between devices with their start and end apart: 8, of which 5 were waited for; matrix products, arithmetic and copies ran while one was open for 0% of the time, Pallas kernels for 7%

profile of v2, /device:TPU:1, one launch (start us, length us, event | category | flops | bytes accessed | tf_op | source)
XLA Modules:
  0.0 168.1 jit_solution(14933105787688057577)
XLA Ops:
  0.7 10.8 %all-gather = bf16[512,128]{1,0:T(8,128)(2,1)S(1)} all-gather(bf16[128,128]{1,0:T(8,128)(2,1)} %param.12), channel_id=2, replica_groups=mesh['space'=128,'col'=4] {'col'}, dimensions={0}, use_global_device_ids=true | all-gather | bytes 163840 | tf_op jit(solution)/shard_map/all_gather | solution.py:279
  11.5 0.7 copy-done.5
  12.1 0.8 copy-done.1
  13.0 1.3 shard_map.163
  14.3 22.6 %all-to-all-start.1 = ((bf16[128,8,128]{2,1,0:T(8,128)(2,1)}), bf16[128,8,128]{2,1,0:T(8,128)(2,1)S(1)}, u32[]{:S(2)}, u32[]{:S(2)}) async-start(bf16[128,8,128]{2,1,0:T(8,128)(2,1)} %bitcast.9), calls=%async_computation.1 | async-start | bytes 524288 | tf_op jit(solution)/shard_map/all_to_all | solution.py:285
  36.9 0.0 copy-start.8
  37.0 0.0 copy-start.9
  37.0 0.0 copy-start.10
  37.0 0.0 copy-start.11
  37.0 12.1 %all-gather.1 = bf16[2560,128]{1,0:T(8,128)(2,1)S(1)} all-gather(bf16[640,128]{1,0:T(8,128)(2,1)S(1)} %shard_map.164), channel_id=3, replica_groups=mesh['space'=128,'col'=4] {'col'}, dimensions={0}, use_global_device_ids=true | all-gather | bytes 819200 | tf_op jit(solution)/shard_map/all_gather | solution.py:289
  49.1 4.6 %shard_map.165 = (bf16[128,128]{1,0:T(8,128)(2,1)S(1)}, f32[128,128]{1,0:T(8,128)S(1)}, bf16[1024,128]{1,0:T(8,128)(2,1)}) custom-call(bf16[4,640,128]{2,1,0:T(8,128)(2,1)S(1)} %bitcast.19, bf16[64,4096]{1,0:T(8,128)(2,1)S(1)} %bitcast.26, bf16[64,128]{1,0:T(8,128)(2,1)S(1)} %copy-done.9, s32[32,128]{1,0:T(8,128)S(1)} %bitcast.28, s32[32,128]{1,0:T(8,128)S(1)} %bitcast.30), custom_call_target="tpu_custom_call" | custom-call | flops 1207959552 | bytes 1589248 | tf_op jit(solution)/shard_map/pallas_call | solution.py:21
  53.6 3.7 %all-to-all-done.1 = bf16[128,8,128]{2,1,0:T(8,128)(2,1)S(1)} async-done(((bf16[128,8,128]{2,1,0:T(8,128)(2,1)}), bf16[128,8,128]{2,1,0:T(8,128)(2,1)S(1)}, u32[]{:S(2)}, u32[]{:S(2)}) %all-to-all-start.1) | async-done | bytes 262176 | tf_op jit(solution)/shard_map/all_to_all | solution.py:285
  57.4 13.6 %all-to-all-start = ((bf16[128,8,128]{2,1,0:T(8,128)(2,1)}), bf16[128,8,128]{2,1,0:T(8,128)(2,1)S(1)}, u32[]{:S(2)}, u32[]{:S(2)}) async-start(bf16[128,8,128]{2,1,0:T(8,128)(2,1)} %bitcast.7), calls=%async_computation | async-start | bytes 524288 | tf_op jit(solution)/shard_map/all_to_all | solution.py:297
  70.9 6.4 %shard_map.166 = (bf16[128,128]{1,0:T(8,128)(2,1)S(1)}, f32[64,128]{1,0:T(8,128)S(1)}) custom-call(bf16[128,128]{1,0:T(8,128)(2,1)S(1)} %get-tuple-element.32.after_ref.act_ref, bf16[1024,128]{1,0:T(8,128)(2,1)S(1)} %bitcast.21, bf16[128,128]{1,0:T(8,128)(2,1)S(1)} %get-tuple-element.38.gm_ref, bf16[64,4096]{1,0:T(8,128)(2,1)S(1)} %bitcast.27, ...), custom_call_target="tpu_custom_call" | custom-call | flops 1207959552 | bytes 966656 | tf_op jit(solution)/shard_map/pallas_call | solution.py:21
  77.4 0.0 copy-start.2
  77.4 10.1 %all-gather.2 = bf16[512,128]{1,0:T(8,128)(2,1)S(1)} all-gather(bf16[128,128]{1,0:T(8,128)(2,1)S(1)} %get-tuple-element.39), channel_id=4, replica_groups=mesh['space'=128,'col'=4] {'col'}, dimensions={0}, use_global_device_ids=true | all-gather | bytes 163840 | tf_op jit(solution)/shard_map/all_gather | solution.py:307
  87.5 4.0 %all-to-all-done = bf16[128,8,128]{2,1,0:T(8,128)(2,1)S(1)} async-done(((bf16[128,8,128]{2,1,0:T(8,128)(2,1)}), bf16[128,8,128]{2,1,0:T(8,128)(2,1)S(1)}, u32[]{:S(2)}, u32[]{:S(2)}) %all-to-all-start) | async-done | bytes 262176 | tf_op jit(solution)/shard_map/all_to_all | solution.py:297
  91.5 0.8 shard_map.167
  92.3 2.4 %collective-permute-start.3 = (bf16[704,128]{1,0:T(8,128)(2,1)S(1)}, bf16[704,128]{1,0:T(8,128)(2,1)S(1)}, u32[]{:S(2)}, u32[]{:S(2)}) collective-permute-start(bf16[704,128]{1,0:T(8,128)(2,1)S(1)} %get-tuple-element.49), channel_id=1, source_target_pairs={{0,4},{4,0},{8,12},{12,8},{16,20},{20,16},{24,28},{28,24},{32,36},... | collective-permute-start | bytes 540680 | tf_op jit(solution)/shard_map/ppermute | solution.py:253
  94.7 1.0 collective-permute-done.3.got_ref
  95.8 4.2 %collective-permute-start.4 = (bf16[352,128]{1,0:T(8,128)(2,1)S(1)}, bf16[352,128]{1,0:T(8,128)(2,1)S(1)}, u32[]{:S(2)}, u32[]{:S(2)}) collective-permute-start(bf16[352,128]{1,0:T(8,128)(2,1)S(1)} %get-tuple-element.51), channel_id=1, source_target_pairs={{0,8},{4,12},{8,0},{12,4},{16,24},{20,28},{24,16},{28,20},{32,40},... | collective-permute-start | bytes 270344 | tf_op jit(solution)/shard_map/ppermute | solution.py:253
  100.0 3.3 %collective-permute-start = (bf16[160,128]{1,0:T(8,128)(2,1)S(1)}, bf16[160,128]{1,0:T(8,128)(2,1)S(1)}, u32[]{:S(2)}, u32[]{:S(2)}) collective-permute-start(bf16[160,128]{1,0:T(8,128)(2,1)S(1)} %get-tuple-element.43), channel_id=1, source_target_pairs={{0,1},{1,0},{2,3},{3,2},{4,5},{5,4},{6,7},{7,6},{8,9},{9,8},{10,11... | collective-permute-start | bytes 122888 | tf_op jit(solution)/shard_map/ppermute | solution.py:249
  103.3 1.4 collective-permute-done.got1.after_ref
  104.7 4.7 %collective-permute-start.5 = (bf16[176,128]{1,0:T(8,128)(2,1)S(1)}, bf16[176,128]{1,0:T(8,128)(2,1)S(1)}, u32[]{:S(2)}, u32[]{:S(2)}) collective-permute-start(bf16[176,128]{1,0:T(8,128)(2,1)S(1)} %get-tuple-element.53), channel_id=1, source_target_pairs={{0,16},{4,20},{8,24},{12,28},{16,0},{20,4},{24,8},{28,12},{32,48},... | collective-permute-start | bytes 135176 | tf_op jit(solution)/shard_map/ppermute | solution.py:253
  109.4 4.2 %collective-permute-start.1 = (bf16[160,128]{1,0:T(8,128)(2,1)S(1)}, bf16[160,128]{1,0:T(8,128)(2,1)S(1)}, u32[]{:S(2)}, u32[]{:S(2)}) collective-permute-start(bf16[160,128]{1,0:T(8,128)(2,1)S(1)} %get-tuple-element.44), channel_id=1, source_target_pairs={{0,2},{1,3},{2,0},{3,1},{4,6},{5,7},{6,4},{7,5},{8,10},{9,11},{10,... | collective-permute-start | bytes 122888 | tf_op jit(solution)/shard_map/ppermute | solution.py:249
  113.7 3.4 %collective-permute-start.2 = (bf16[160,128]{1,0:T(8,128)(2,1)S(1)}, bf16[160,128]{1,0:T(8,128)(2,1)S(1)}, u32[]{:S(2)}, u32[]{:S(2)}) collective-permute-start(bf16[160,128]{1,0:T(8,128)(2,1)S(1)} %get-tuple-element.45), channel_id=1, source_target_pairs={{0,3},{1,2},{2,1},{3,0},{4,7},{5,6},{6,5},{7,4},{8,11},{9,10},{10,... | collective-permute-start | bytes 122888 | tf_op jit(solution)/shard_map/ppermute | solution.py:249
  117.0 2.6 %collective-permute-done.2.got3.after3 = bf16[160,128]{1,0:T(8,128)(2,1)S(1)} collective-permute-done((bf16[160,128]{1,0:T(8,128)(2,1)S(1)}, bf16[160,128]{1,0:T(8,128)(2,1)S(1)}, u32[]{:S(2)}, u32[]{:S(2)}) %collective-permute-start.2) | collective-permute-done | bytes 40992 | tf_op jit(solution)/shard_map/ppermute | solution.py:249
  119.6 0.6 shard_map.168
  120.3 23.6 %all-gather.3 = bf16[2816,128]{1,0:T(8,128)(2,1)S(1)} all-gather(bf16[176,128]{1,0:T(8,128)(2,1)S(1)} %shard_map.171), channel_id=5, replica_groups={{0,32,64,96,128,160,192,224,256,288,320,352,384,416,448,480},{484,452,4..., dimensions={0}, use_global_device_ids=true | all-gather | bytes 765952 | tf_op jit(solution)/shard_map/all_gather | solution.py:339
  143.9 0.1 shard_map.172
  144.0 23.2 %all-gather.4 = bf16[1408,128]{1,0:T(8,128)(2,1)S(1)} all-gather(bf16[176,128]{1,0:T(8,128)(2,1)S(1)} %shard_map.172), channel_id=6, replica_groups={{0,4,8,12,16,20,24,28},{32,36,40,44,48,52,56,60},{64,68,72,76,80,84,88,..., dimensions={0}, use_global_device_ids=true | all-gather | bytes 405504 | tf_op jit(solution)/shard_map/all_gather | solution.py:342
  167.2 0.9 shard_map.173
  (24 shorter events, 0.1 us)
Async XLA Ops:
  0.6 10.8 %copy-start = (bf16[512,128]{1,0:T(8,128)(2,1)S(1)}, bf16[512,128]{1,0:T(8,128)(2,1)}, u32[]{:S(2)}) copy-start(bf16[512,128]{1,0:T(8,128)(2,1)} %win_ref.3) | copy-start | bytes 393220
  0.6 10.8 %copy-start.6 = (bf16[8,256]{1,0:T(8,128)(2,1)S(1)}, bf16[8,256]{1,0:T(8,128)(2,1)}, u32[]{:S(2)}) copy-start(bf16[8,256]{1,0:T(8,128)(2,1)} %atom_ref.1) | copy-start | bytes 12292
  11.5 0.7 copy-start.5
  11.5 0.7 copy-start.7
  12.1 0.8 copy-start.1
  14.3 22.6 %copy-start.3 = (bf16[512,128]{1,0:T(8,128)(2,1)S(1)}, bf16[512,128]{1,0:T(8,128)(2,1)}, u32[]{:S(2)}) copy-start(bf16[512,128]{1,0:T(8,128)(2,1)} %wout_ref.1) | copy-start | bytes 393220
  14.3 22.6 %copy-start.4 = (bf16[128,128]{1,0:T(8,128)(2,1)S(1)}, bf16[128,128]{1,0:T(8,128)(2,1)}, u32[]{:S(2)}) copy-start(bf16[128,128]{1,0:T(8,128)(2,1)} %cot_ref.3) | copy-start | bytes 98308
  14.3 43.1 %all-to-all-start.1 = ((bf16[128,8,128]{2,1,0:T(8,128)(2,1)}), bf16[128,8,128]{2,1,0:T(8,128)(2,1)S(1)}, u32[]{:S(2)}, u32[]{:S(2)}) async-start(bf16[128,8,128]{2,1,0:T(8,128)(2,1)} %bitcast.9), calls=%async_computation.1 | async-start | bytes 524288 | tf_op jit(solution)/shard_map/all_to_all | solution.py:285
  36.9 12.1 %copy-start.8 = (bf16[4096,64]{0,1:T(8,128)(2,1)S(1)}, bf16[4096,64]{0,1:T(8,128)(2,1)}, u32[]{:S(2)}) copy-start(bf16[4096,64]{0,1:T(8,128)(2,1)} %param.15) | copy-start | bytes 1572868
  37.0 12.1 %copy-start.9 = (bf16[64,128]{1,0:T(8,128)(2,1)S(1)}, bf16[64,128]{1,0:T(8,128)(2,1)}, u32[]{:S(2)}) copy-start(bf16[64,128]{1,0:T(8,128)(2,1)} %wb_ref.3) | copy-start | bytes 49156
  37.0 12.1 %copy-start.10 = (s32[4096]{0:T(1024)S(1)}, s32[4096]{0:T(1024)}, u32[]{:S(2)}) copy-start(s32[4096]{0:T(1024)} %param.21) | copy-start | bytes 49156
  37.0 12.1 %copy-start.11 = (s32[4096]{0:T(1024)S(1)}, s32[4096]{0:T(1024)}, u32[]{:S(2)}) copy-start(s32[4096]{0:T(1024)} %param.22) | copy-start | bytes 49156
  57.4 34.1 %all-to-all-start = ((bf16[128,8,128]{2,1,0:T(8,128)(2,1)}), bf16[128,8,128]{2,1,0:T(8,128)(2,1)S(1)}, u32[]{:S(2)}, u32[]{:S(2)}) async-start(bf16[128,8,128]{2,1,0:T(8,128)(2,1)} %bitcast.7), calls=%async_computation | async-start | bytes 524288 | tf_op jit(solution)/shard_map/all_to_all | solution.py:297
  77.4 14.1 %copy-start.2 = (bf16[256,128]{1,0:T(8,128)(2,1)S(1)}, bf16[256,128]{1,0:T(8,128)(2,1)}, u32[]{:S(2)}) copy-start(bf16[256,128]{1,0:T(8,128)(2,1)} %watom_ref.3) | copy-start | bytes 196612
  92.3 3.4 %collective-permute-start.3 = (bf16[704,128]{1,0:T(8,128)(2,1)S(1)}, bf16[704,128]{1,0:T(8,128)(2,1)S(1)}, u32[]{:S(2)}, u32[]{:S(2)}) collective-permute-start(bf16[704,128]{1,0:T(8,128)(2,1)S(1)} %get-tuple-element.49), channel_id=1, source_target_pairs={{0,4},{4,0},{8,12},{12,8},{16,20},{20,16},{24,28},{28,24},{32,36},... | collective-permute-start | bytes 540680 | tf_op jit(solution)/shard_map/ppermute | solution.py:253
  95.8 8.9 %collective-permute-start.4 = (bf16[352,128]{1,0:T(8,128)(2,1)S(1)}, bf16[352,128]{1,0:T(8,128)(2,1)S(1)}, u32[]{:S(2)}, u32[]{:S(2)}) collective-permute-start(bf16[352,128]{1,0:T(8,128)(2,1)S(1)} %get-tuple-element.51), channel_id=1, source_target_pairs={{0,8},{4,12},{8,0},{12,4},{16,24},{20,28},{24,16},{28,20},{32,40},... | collective-permute-start | bytes 270344 | tf_op jit(solution)/shard_map/ppermute | solution.py:253
  100.0 4.7 %collective-permute-start = (bf16[160,128]{1,0:T(8,128)(2,1)S(1)}, bf16[160,128]{1,0:T(8,128)(2,1)S(1)}, u32[]{:S(2)}, u32[]{:S(2)}) collective-permute-start(bf16[160,128]{1,0:T(8,128)(2,1)S(1)} %get-tuple-element.43), channel_id=1, source_target_pairs={{0,1},{1,0},{2,3},{3,2},{4,5},{5,4},{6,7},{7,6},{8,9},{9,8},{10,11... | collective-permute-start | bytes 122888 | tf_op jit(solution)/shard_map/ppermute | solution.py:249
  104.7 15.5 %collective-permute-start.5 = (bf16[176,128]{1,0:T(8,128)(2,1)S(1)}, bf16[176,128]{1,0:T(8,128)(2,1)S(1)}, u32[]{:S(2)}, u32[]{:S(2)}) collective-permute-start(bf16[176,128]{1,0:T(8,128)(2,1)S(1)} %get-tuple-element.53), channel_id=1, source_target_pairs={{0,16},{4,20},{8,24},{12,28},{16,0},{20,4},{24,8},{28,12},{32,48},... | collective-permute-start | bytes 135176 | tf_op jit(solution)/shard_map/ppermute | solution.py:253
  109.4 7.6 %collective-permute-start.1 = (bf16[160,128]{1,0:T(8,128)(2,1)S(1)}, bf16[160,128]{1,0:T(8,128)(2,1)S(1)}, u32[]{:S(2)}, u32[]{:S(2)}) collective-permute-start(bf16[160,128]{1,0:T(8,128)(2,1)S(1)} %get-tuple-element.44), channel_id=1, source_target_pairs={{0,2},{1,3},{2,0},{3,1},{4,6},{5,7},{6,4},{7,5},{8,10},{9,11},{10,... | collective-permute-start | bytes 122888 | tf_op jit(solution)/shard_map/ppermute | solution.py:249
  113.7 6.0 %collective-permute-start.2 = (bf16[160,128]{1,0:T(8,128)(2,1)S(1)}, bf16[160,128]{1,0:T(8,128)(2,1)S(1)}, u32[]{:S(2)}, u32[]{:S(2)}) collective-permute-start(bf16[160,128]{1,0:T(8,128)(2,1)S(1)} %get-tuple-element.45), channel_id=1, source_target_pairs={{0,3},{1,2},{2,1},{3,0},{4,7},{5,6},{6,5},{7,4},{8,11},{9,10},{10,... | collective-permute-start | bytes 122888 | tf_op jit(solution)/shard_map/ppermute | solution.py:249

commit v3 on v2

v3 whole, which is shorter than its diff:
```python
import functools
import math

import jax
import jax.numpy as jnp
from jax import lax
from jax.experimental import pallas as pl
from jax.experimental.pallas import tpu as pltpu
from jax.sharding import PartitionSpec as P

F32 = jnp.float32
BF16 = jnp.bfloat16
VMEM = pl.BlockSpec(memory_space=pltpu.VMEM)
ROWS = 1408
STEP = 512


def call(kernel, outs, *args, scratch=(), flops=0, limit=20):
    total = sum(math.prod(o.shape) * o.dtype.itemsize for o in outs)
    total += sum(a.size * a.dtype.itemsize for a in args)
    return pl.pallas_call(
        kernel,
        out_shape=list(outs),
        in_specs=[VMEM] * len(args),
        out_specs=[VMEM] * len(outs),
        scratch_shapes=list(scratch),
        compiler_params=pltpu.CompilerParams(vmem_limit_bytes=limit * 1024 * 1024),
        cost_estimate=pl.CostEstimate(flops=flops, bytes_accessed=total, transcendentals=0),
    )(*args)


def shape(*dims, dtype=F32):
    return jax.ShapeDtypeStruct(dims, dtype)


def dot(a, b, dims=((1,), (0,))):
    return lax.dot_general(a, b, (dims, ((), ())), preferred_element_type=F32)


def dot_nt(a, b):
    return dot(a, b, ((1,), (1,)))


def dot_tn(a, b):
    return dot(a, b, ((0,), (0,)))


def one_hot(mask):
    return jnp.where(mask, 1.0, 0.0).astype(BF16)


def iota(rows, lanes, axis):
    return lax.broadcasted_iota(jnp.int32, (rows, lanes), axis)


def bit_of(level):
    return lax.rem(lax.axis_index("space") // (1 << level), 2)


def sigmoid(value):
    return 1.0 / (1.0 + jnp.exp(-value))


def pack_kernel(edge_ref, cot_ref, wout_ref, out_ref):
    out_ref[:128, :] = edge_ref[...]
    out_ref[128:256, :] = cot_ref[...]
    out_ref[256:, :] = wout_ref[...]


def pack_weights_kernel(win_ref, watom_ref, after_ref, out_ref):
    out_ref[:512, :] = win_ref[...]
    out_ref[512:, :] = watom_ref[...]


def target_mask(target_ref, lines):
    return jnp.concatenate(
        [one_hot(iota(128, 128, 0) == target_ref[i : i + 1, :]) for i in lines], axis=1
    )


def steps(source_ref):
    for c in range(source_ref.shape[0] * 128 // STEP):
        yield slice(c * STEP, (c + 1) * STEP), range(c * STEP // 128, (c + 1) * STEP // 128)


def front_kernel(
    all_ref, atom_ref, win_ref, watom_ref, index_ref, send_ref, basis_ref, wb_ref, source_ref,
    target_ref,
    pre_ref, act_ref, ae_ref, gm_ref, own_ref, both_ref, acc_ref,
):
    at = one_hot(iota(8, 128, 0) == index_ref[...])
    atom_edge = dot_tn(at, atom_ref[...]).astype(BF16)
    ae_ref[...] = atom_edge
    pre = dot(atom_edge, watom_ref[...])
    mine = pl.ds(pl.multiple_of(lax.axis_index("col") * 128 + 256, 128), 128)
    total = jnp.zeros((128, 128), F32)
    for c in range(4):
        pre = pre + dot(all_ref[c, :128, :], win_ref[c * 128 : (c + 1) * 128, :])
        total = total + dot_nt(all_ref[c, 128:256, :], all_ref[c, mine, :])
    pre_ref[...] = pre
    act = (pre * sigmoid(pre)).astype(BF16)
    act_ref[...] = act
    gm = total.astype(BF16)
    gm_ref[...] = gm
    wb = wb_ref[...]
    rows = acc_ref.shape[0]
    for span, lines in steps(source_ref):
        exact = dot_tn(target_mask(target_ref, lines), gm) * dot_tn(basis_ref[:, span], wb)
        high = exact.astype(BF16)
        low = (exact - high.astype(F32)).astype(BF16)
        put = jnp.concatenate(
            [one_hot(iota(rows, 128, 0) == source_ref[i : i + 1, :]) for i in lines], axis=1
        )
        two = dot(put, jnp.concatenate([high, low], axis=1))
        part = two[:, :128] + two[:, 128:]
        if span.start == 0:
            acc_ref[...] = part
        else:
            acc_ref[...] += part
    own_ref[...] = acc_ref[:128, :]
    for i in range(8):
        pick = one_hot(iota(128, 128, 0) == send_ref[i : i + 1, :])
        outgoing = dot_tn(pick, act).reshape(16, 8, 128)
        back = acc_ref[(i + 1) * 128 : (i + 2) * 128, :].reshape(16, 8, 128)
        both_ref[i * 256 : (i + 1) * 256, :] = (
            jnp.concatenate([outgoing, back], axis=1).reshape(256, 128).astype(BF16)
        )


def gather_kernel(
    act_ref, in_ref, own_ref, pre_ref, send_ref, gm_ref, basis_ref, wb_ref, source_ref, target_ref,
    after_ref,
    pair_ref, bw_ref, ext_ref,
):
    got = in_ref[...].astype(F32).reshape(-1, 16, 128)
    ext_ref[:128, :] = act_ref[...]
    ext_ref[128:, :] = got[:, :8, :].reshape(-1, 128).astype(BF16)
    back = got[:, 8:, :].reshape(-1, 128).astype(BF16)
    ga = own_ref[...]
    for i in range(8):
        put = one_hot(iota(128, 128, 0) == send_ref[i : i + 1, :])
        ga = ga + dot(put, back[i * 128 : (i + 1) * 128, :])
    pre = pre_ref[...]
    sig = sigmoid(pre)
    pair_ref[128:, :] = (ga * (sig * (1.0 + pre * (1.0 - sig)))).astype(BF16)
    ext = ext_ref[...]
    msg = jnp.zeros((128, 128), F32)
    bw = jnp.zeros(bw_ref.shape, F32)
    gm = gm_ref[...]
    wb = wb_ref[...]
    for span, lines in steps(source_ref):
        basis = basis_ref[:, span]
        mask = target_mask(target_ref, lines)
        cols = jnp.concatenate(
            [jnp.broadcast_to(source_ref[i : i + 1, :], (128, 128)).T for i in lines], axis=0
        )
        pick = jnp.concatenate(
            [
                one_hot(cols == iota(STEP, 128, 1) + 128 * k)
                for k in range(ext_ref.shape[0] // 128)
            ],
            axis=1,
        )
        z = dot(pick, ext)
        msg = msg + dot(mask, (dot_tn(basis, wb) * z).astype(BF16))
        bw = bw + dot(basis, (dot_tn(mask, gm) * z).astype(BF16))
    pair_ref[:128, :] = msg.astype(BF16)
    bw_ref[...] = bw


def weight_kernel(all_ref, pair_all, pair_ref, ae_ref, cot_ref, bw_ref, out_ref, keep_ref, acc_ref):
    gp = pair_ref[128:, :]
    cot = cot_ref[...]
    for c in range(4):
        acc_ref[c * 128 : (c + 1) * 128, :] = dot_tn(all_ref[c, :128, :], gp)
        acc_ref[768 + c * 128 : 896 + c * 128, :] = dot_tn(pair_all[c, :128, :], cot)
    acc_ref[512:768, :] = dot_tn(ae_ref[...], gp)
    acc_ref[1280:1344, :] = bw_ref[...]
    acc_ref[1344:, :] = jnp.zeros((ROWS - 1344, 128), F32)
    half = ROWS // 2
    mine = pl.multiple_of(bit_of(0) * half, 16)
    other = pl.multiple_of(half - mine, 16)
    keep_ref[...] = acc_ref[pl.ds(mine, half), :]
    out_ref[...] = acc_ref[pl.ds(other, half), :].astype(BF16)


def edge_out_kernel(pair_all, weights_ref, index_ref, edge_ref, atom_ref):
    mine = pl.ds(pl.multiple_of(lax.axis_index("col") * 128, 128), 128)
    at = one_hot(iota(8, 128, 0) == index_ref[...])
    edge = jnp.zeros((128, 128), F32)
    atom = jnp.zeros((8, 256), F32)
    for c in range(4):
        gp = pair_all[c, 128:, :]
        edge = edge + dot_nt(gp, weights_ref[c, mine, :])
        total = dot(at, gp)
        high = total.astype(BF16)
        low = (total - high.astype(F32)).astype(BF16)
        atom = atom + dot_nt(high, weights_ref[c, 512:, :]) + dot_nt(low, weights_ref[c, 512:, :])
    edge_ref[...] = edge.astype(BF16)
    atom_ref[...] = atom


def halve_kernel(level, keep_ref, got_ref, send_ref, own_ref):
    half = send_ref.shape[0]
    mine = pl.multiple_of(bit_of(level) * half, 16)
    other = pl.multiple_of(half - mine, 16)
    send_ref[...] = (
        keep_ref[pl.ds(other, half), :] + got_ref[pl.ds(other, half), :].astype(F32)
    ).astype(BF16)
    own_ref[...] = keep_ref[pl.ds(mine, half), :] + got_ref[pl.ds(mine, half), :].astype(F32)


def add_kernel(own_ref, got_ref, after_ref, out_ref):
    out_ref[...] = (own_ref[...] + got_ref[...].astype(F32)).astype(BF16)


def z_sum_kernel(all_ref, out_ref):
    total = all_ref[0].astype(F32)
    for i in range(1, all_ref.shape[0]):
        total = total + all_ref[i].astype(F32)
    out_ref[...] = total.astype(BF16)


def final_kernel(scale, all_ref, win_ref, watom_ref, wb_ref, wout_ref, acc_ref):
    rows = all_ref.shape[1]
    for g in range(8):
        place = ((g % 2) * 4 + (g // 2 % 2) * 2 + g // 4) * rows
        acc_ref[place : place + rows, :] = all_ref[g].astype(F32) * scale
    win_ref[...] = acc_ref[:512, :]
    watom_ref[...] = acc_ref[512:768, :]
    wout_ref[...] = acc_ref[768:1280, :]
    wb_ref[...] = acc_ref[1280:1344, :]


def space_swap(array, distance, extent):
    return lax.ppermute(array, "space", [(i, i ^ distance) for i in range(extent)])


def body(
    edge_embed,
    atom_embed,
    cotangent,
    trip_basis,
    weight_in,
    weight_atom,
    weight_basis,
    weight_out,
    atom_index,
    trip_source,
    trip_target,
    send_rows,
):
    extent = lax.axis_size("space")
    grad_scale = 1.0 / math.sqrt(edge_embed.shape[0] * extent)
    half = dict(dtype=BF16)
    source = trip_source.reshape(-1, 128)
    target = trip_target.reshape(-1, 128)
    send = send_rows.reshape(8, 128)
    index = atom_index.reshape(1, 128)

    basis = trip_basis.T
    (packed,) = call(
        pack_kernel, [shape(768, 128, **half)], edge_embed, cotangent, weight_out, limit=58
    )
    col_all = lax.all_gather(packed, "col")
    preact, active, atom_edge, grad_msg, grad_own, both = call(
        front_kernel,
        [
            shape(128, 128), shape(128, 128, **half), shape(128, 256, **half),
            shape(128, 128, **half), shape(128, 128), shape(2048, 128, **half),
        ],
        col_all, atom_embed, weight_in, weight_atom, index, send, basis, weight_basis, source, target,
        scratch=[pltpu.VMEM((1152, 128), F32)],
        flops=2 * 4096 * 1152 * 128,
        limit=58,
    )
    both = lax.all_to_all(
        both.reshape(extent, 16, 128), "space", split_axis=0, concat_axis=0, tiled=True
    ).reshape(2048, 128)
    (weights,) = call(
        pack_weights_kernel, [shape(768, 128, **half)], weight_in, weight_atom, grad_own
    )
    weights = lax.all_gather(weights, "col")
    pair, grad_bw = call(
        gather_kernel,
        [shape(256, 128, **half), shape(64, 128)],
        active, both, grad_own, preact, send, grad_msg, basis, weight_basis, source, target, weights,
        scratch=[pltpu.VMEM((1152, 128), BF16)],
        flops=2 * 4096 * 1152 * 128,
        limit=58,
    )
    pair_all = lax.all_gather(pair, "col")
    out, keep = call(
        weight_kernel,
        [shape(ROWS // 2, 128, **half), shape(ROWS // 2, 128)],
        col_all, pair_all, pair, atom_edge, cotangent, grad_bw,
        scratch=[pltpu.VMEM((ROWS, 128), F32)],
    )
    grad_edge, grad_atom = call(
        edge_out_kernel, [shape(128, 128, **half), shape(8, 256)], pair_all, weights, index
    )
    rows = ROWS // 2
    for level in (1, 2):
        rows //= 2
        got = space_swap(out, 1 << (level - 1), extent)
        out, keep = call(
            functools.partial(halve_kernel, level),
            [shape(rows, 128, **half), shape(rows, 128)],
            keep, got,
        )
    (out,) = call(
        add_kernel, [shape(rows, 128, **half)], keep, space_swap(out, 4, extent), grad_atom
    )
    depth = extent // 8
    groups = [[z * 8 + g for z in range(depth)] for g in range(8)]
    out = lax.all_gather(out, "space", axis_index_groups=groups)
    (out,) = call(z_sum_kernel, [shape(rows, 128, **half)], out)
    groups = [[z * 8 + g for g in range(8)] for z in range(depth)]
    out = lax.all_gather(out, "space", axis_index_groups=groups)
    sum_in, sum_atom, sum_basis, sum_out = call(
        functools.partial(final_kernel, grad_scale),
        [shape(512, 128), shape(256, 128), shape(64, 128), shape(512, 128)],
        out,
        scratch=[pltpu.VMEM((ROWS, 128), F32)],
    )
    return grad_edge, grad_atom, sum_in, sum_atom, sum_basis, sum_out


def solution(mesh):
    placed = (
        P("space", "col"),
        P("space", None),
        P("space", "col"),
        P("space", None),
        P(None, "col"),
        P(None, "col"),
        P(None, "col"),
        P(None, "col"),
        P("space"),
        P("space"),
        P("space"),
        P("space", None),
    )
    return jax.shard_map(
        body,
        mesh=mesh,
        in_specs=placed,
        out_specs=(
            P("space", "col"),
            P("space", None),
            P(None, "col"),
            P(None, "col"),
            P(None, "col"),
            P(None, "col"),
        ),
        check_vma=False,
    )
```

time: 169 us -> 166 us (0.982)
  starting transfers between devices: 58.3 us -> 37.6 us
  waiting for transfers between devices: 12.7 us -> 23.2 us
  Pallas kernels: 14.8 us -> 19.3 us
  blocking collectives: 79.8 us -> 82.8 us
    all_to_all x2 -> x1, starting transfers between devices: 36.1 us -> 22.7 us  [body(): lax.all_to_all(both.reshape(extent, 16, 128), 'space', split_axis=0, conc...]
    all_to_all x2 -> x1, waiting for transfers between devices: 7.7 us -> 19 us  [body(): lax.all_to_all(both.reshape(extent, 16, 128), 'space', split_axis=0, conc...]
    ppermute x3 -> x0, starting transfers between devices: 10.9 us -> none  [col_swap(): return lax.ppermute(array, 'col', [(i, i ^ distance) for i in range(4)])]
    pallas_call x11, Pallas kernels: 14.8 us -> 19.3 us  [call(): pl.pallas_call(kernel, out_shape=list(outs), in_specs=[VMEM] * len(args),...]
    ppermute x3 -> x0, waiting for transfers between devices: 4.01 us -> none  [col_swap(): return lax.ppermute(array, 'col', [(i, i ^ distance) for i in range(4)])]
    ppermute x3, starting transfers between devices: 11.2 us -> 14.9 us  [space_swap(): lax.ppermute(array, 'space', [(i, i ^ distance) for i in range(extent)])]
    ppermute x3, waiting for transfers between devices: 1.03 us -> 4.11 us  [space_swap(): lax.ppermute(array, 'space', [(i, i ^ distance) for i in range(extent)])]
    all_gather x3, blocking collectives: 33 us -> 35.5 us  [the longest x1 14 us: body(): col_all = lax.all_gather(packed, 'col')]
  transfers between devices with their start and end apart: 8 -> 4, of which waited for: 5 -> 4; matrix products, arithmetic and copies ran while one was open for 0% -> 0% of each run, Pallas kernels for 7% -> 1%
where the time goes in v3:
time: 166 us; the launch traced here: 165 us
  blocking collectives  82.8 us (50%)
  starting transfers between devices  37.6 us (23%)
  waiting for transfers between devices  23.2 us (14%)
  Pallas kernels  19.3 us (12%)
    all_gather x2, blocking collectives, body(): out = lax.all_gather(out, 'space', axis_index_groups=groups)  47.4 us
    all_to_all x1, starting transfers between devices, body(): lax.all_to_all(both.reshape(extent, 16, 128), 'space', split_axis=0, conc...  22.7 us
    pallas_call x11, Pallas kernels, call(): pl.pallas_call(kernel, out_shape=list(outs), in_specs=[VMEM] * len(args),...  19.3 us
    all_to_all x1, waiting for transfers between devices, body(): lax.all_to_all(both.reshape(extent, 16, 128), 'space', split_axis=0, conc...  19 us
    ppermute x3, starting transfers between devices, space_swap(): lax.ppermute(array, 'space', [(i, i ^ distance) for i in range(extent)])  14.9 us
    all_gather x1, blocking collectives, body(): col_all = lax.all_gather(packed, 'col')  14 us
    all_gather x1, blocking collectives, body(): weights = lax.all_gather(weights, 'col')  11.7 us
    all_gather x1, blocking collectives, body(): pair_all = lax.all_gather(pair, 'col')  9.71 us
  transfers between devices with their start and end apart: 4, of which 4 were waited for; matrix products, arithmetic and copies ran while one was open for 0% of the time, Pallas kernels for 1%

profile of v3, /device:TPU:1, one launch (start us, length us, event | category | flops | bytes accessed | tf_op | source)
XLA Modules:
  0.0 165.2 jit_solution(3524669749661660248)
XLA Ops:
  0.6 1.6 shard_map.163
  2.3 14.0 %all-gather = bf16[3072,128]{1,0:T(8,128)(2,1)} all-gather(bf16[768,128]{1,0:T(8,128)(2,1)} %shard_map.163), channel_id=2, replica_groups=mesh['space'=128,'col'=4] {'col'}, dimensions={0}, use_global_device_ids=true | all-gather | bytes 983040 | tf_op jit(solution)/shard_map/all_gather | solution.py:265
  16.3 6.5 %shard_map.164 = (f32[128,128]{1,0:T(8,128)}, bf16[128,128]{1,0:T(8,128)(2,1)}, bf16[128,256]{1,0:T(8,128)(2,1)}, bf16[128,128]{1,0:T(8,128)(2,1)}, f32[128,128]{1,0:T(8,128)}, /*index=5*/bf16[2048,128]{1,0:T(8,128)(2,1)}) custom-call(bf16[4,768,128]{2,1,0:T(8,128)(2,1)} %bitcast.12, bf16[8,256]{1,0:T(8,128)(2,1)} %atom_ref.1, bf16[512,128]{1,0:T(8,128)(2,1)} %win_ref.3, ...), custom_call_target="tpu_custom_call" | custom-call | flops 1207959552 | bytes 2351616 | tf_op jit(solution)/shard_map/pallas_call | solution.py:21
  22.8 0.0 copy-start.7
  22.8 22.7 %all-to-all-start = ((bf16[128,16,128]{2,1,0:T(8,128)(2,1)}), bf16[128,16,128]{2,1,0:T(8,128)(2,1)S(1)}, u32[]{:S(2)}, u32[]{:S(2)}) async-start(bf16[128,16,128]{2,1,0:T(8,128)(2,1)} %bitcast.23), calls=%async_computation | async-start | bytes 1048576 | tf_op jit(solution)/shard_map/all_to_all | solution.py:277
  45.6 0.0 copy-done.3
  45.6 0.0 copy-done.5
  45.6 11.7 %all-gather.1 = bf16[3072,128]{1,0:T(8,128)(2,1)} all-gather(bf16[768,128]{1,0:T(8,128)(2,1)S(1)} %shard_map.165), channel_id=3, replica_groups=mesh['space'=128,'col'=4] {'col'}, dimensions={0}, use_global_device_ids=true | all-gather | bytes 983040 | tf_op jit(solution)/shard_map/all_gather | solution.py:283
  57.3 19.0 %all-to-all-done = bf16[128,16,128]{2,1,0:T(8,128)(2,1)S(1)} async-done(((bf16[128,16,128]{2,1,0:T(8,128)(2,1)}), bf16[128,16,128]{2,1,0:T(8,128)(2,1)S(1)}, u32[]{:S(2)}, u32[]{:S(2)}) %all-to-all-start) | async-done | bytes 524320 | tf_op jit(solution)/shard_map/all_to_all | solution.py:277
  76.4 0.8 copy-done.11
  77.2 8.5 %shard_map.166 = (bf16[256,128]{1,0:T(8,128)(2,1)}, f32[64,128]{1,0:T(8,128)}) custom-call(bf16[128,128]{1,0:T(8,128)(2,1)} %get-tuple-element.26.act_ref, bf16[2048,128]{1,0:T(8,128)(2,1)} %bitcast.22, f32[128,128]{1,0:T(8,128)} %get-tuple-element.28.after_ref.own_ref, f32[128,128]{1,0:T(8,128)} %get-tuple-element.29.pre_ref, s32[8,128]{1,0:T(8,128)} %bitcast.31, ...), custom_call_target="tpu_custom_call" | custom-call | flops 1207959552 | bytes 2183168 | tf_op jit(solution)/shard_map/pallas_call | solution.py:21
  85.7 0.0 copy-start.8
  85.7 9.7 %all-gather.2 = bf16[1024,128]{1,0:T(8,128)(2,1)S(1)} all-gather(bf16[256,128]{1,0:T(8,128)(2,1)} %get-tuple-element.31.pair_ref), channel_id=4, replica_groups=mesh['space'=128,'col'=4] {'col'}, dimensions={0}, use_global_device_ids=true | all-gather | bytes 327680 | tf_op jit(solution)/shard_map/all_gather | solution.py:292
  95.4 0.0 copy-done
  95.4 0.0 copy-done.4
  95.4 0.0 copy-done.6
  95.4 0.0 copy-done.8
  95.5 0.0 copy-start.1
  95.5 0.4 shard_map.168
  95.8 6.2 %collective-permute-start = (bf16[704,128]{1,0:T(8,128)(2,1)S(1)}, bf16[704,128]{1,0:T(8,128)(2,1)S(1)}, u32[]{:S(2)}, u32[]{:S(2)}) collective-permute-start(bf16[704,128]{1,0:T(8,128)(2,1)S(1)} %get-tuple-element.37), channel_id=1, source_target_pairs={{0,4},{4,0},{8,12},{12,8},{16,20},{20,16},{24,28},{28,24},{32,36},... | collective-permute-start | bytes 540680 | tf_op jit(solution)/shard_map/ppermute | solution.py:236
  102.0 1.0 collective-permute-done.got_ref
  103.1 2.8 %collective-permute-start.1 = (bf16[352,128]{1,0:T(8,128)(2,1)S(1)}, bf16[352,128]{1,0:T(8,128)(2,1)S(1)}, u32[]{:S(2)}, u32[]{:S(2)}) collective-permute-start(bf16[352,128]{1,0:T(8,128)(2,1)S(1)} %get-tuple-element.39), channel_id=1, source_target_pairs={{0,8},{4,12},{8,0},{12,4},{16,24},{20,28},{24,16},{28,20},{32,40},... | collective-permute-start | bytes 270344 | tf_op jit(solution)/shard_map/ppermute | solution.py:236
  105.9 2.9 %collective-permute-done.1.got_ref = bf16[352,128]{1,0:T(8,128)(2,1)S(1)} collective-permute-done((bf16[352,128]{1,0:T(8,128)(2,1)S(1)}, bf16[352,128]{1,0:T(8,128)(2,1)S(1)}, u32[]{:S(2)}, u32[]{:S(2)}) %collective-permute-start.1) | collective-permute-done | bytes 90144 | tf_op jit(solution)/shard_map/ppermute | solution.py:236
  108.8 0.0 copy-start.10
  108.9 5.9 %collective-permute-start.2 = (bf16[176,128]{1,0:T(8,128)(2,1)S(1)}, bf16[176,128]{1,0:T(8,128)(2,1)S(1)}, u32[]{:S(2)}, u32[]{:S(2)}) collective-permute-start(bf16[176,128]{1,0:T(8,128)(2,1)S(1)} %get-tuple-element.41), channel_id=1, source_target_pairs={{0,16},{4,20},{8,24},{12,28},{16,0},{20,4},{24,8},{28,12},{32,48},... | collective-permute-start | bytes 135176 | tf_op jit(solution)/shard_map/ppermute | solution.py:236
  114.8 1.2 shard_map.167
  116.0 0.2 collective-permute-done.2.got_ref
  116.2 0.7 copy-done.9
  116.9 25.1 %all-gather.3 = bf16[2816,128]{1,0:T(8,128)(2,1)S(1)} all-gather(bf16[176,128]{1,0:T(8,128)(2,1)S(1)} %shard_map.171), channel_id=5, replica_groups={{0,32,64,96,128,160,192,224,256,288,320,352,384,416,448,480},{4,36,68,1..., dimensions={0}, use_global_device_ids=true | all-gather | bytes 765952 | tf_op jit(solution)/shard_map/all_gather | solution.py:316
  142.1 0.1 shard_map.172
  142.2 22.2 %all-gather.4 = bf16[1408,128]{1,0:T(8,128)(2,1)S(1)} all-gather(bf16[176,128]{1,0:T(8,128)(2,1)S(1)} %shard_map.172), channel_id=6, replica_groups={{0,4,8,12,16,20,24,28},{32,36,40,44,48,52,56,60},{64,68,72,76,80,84,88,..., dimensions={0}, use_global_device_ids=true | all-gather | bytes 405504 | tf_op jit(solution)/shard_map/all_gather | solution.py:319
  164.4 0.9 shard_map.173
  (16 shorter events, 0.1 us)
Async XLA Ops:
  22.8 22.8 %copy-start.3 = (bf16[512,128]{1,0:T(8,128)(2,1)S(1)}, bf16[512,128]{1,0:T(8,128)(2,1)}, u32[]{:S(2)}) copy-start(bf16[512,128]{1,0:T(8,128)(2,1)} %win_ref.3) | copy-start | bytes 393220
  22.8 22.8 %copy-start.5 = (bf16[256,128]{1,0:T(8,128)(2,1)S(1)}, bf16[256,128]{1,0:T(8,128)(2,1)}, u32[]{:S(2)}) copy-start(bf16[256,128]{1,0:T(8,128)(2,1)} %watom_ref.3) | copy-start | bytes 196612
  22.8 22.8 %copy-start.7 = (f32[128,128]{1,0:T(8,128)S(1)}, f32[128,128]{1,0:T(8,128)}, u32[]{:S(2)}) copy-start(f32[128,128]{1,0:T(8,128)} %get-tuple-element.28.after_ref.own_ref) | copy-start | bytes 196612
  22.8 53.6 %all-to-all-start = ((bf16[128,16,128]{2,1,0:T(8,128)(2,1)}), bf16[128,16,128]{2,1,0:T(8,128)(2,1)S(1)}, u32[]{:S(2)}, u32[]{:S(2)}) async-start(bf16[128,16,128]{2,1,0:T(8,128)(2,1)} %bitcast.23), calls=%async_computation | async-start | bytes 1048576 | tf_op jit(solution)/shard_map/all_to_all | solution.py:277
  76.4 0.8 copy-start.11
  77.2 18.2 %copy-start = (bf16[3072,128]{1,0:T(8,128)(2,1)S(1)}, bf16[3072,128]{1,0:T(8,128)(2,1)}, u32[]{:S(2)}) copy-start(bf16[3072,128]{1,0:T(8,128)(2,1)} %all-gather) | copy-start | bytes 2359300
  85.7 9.7 %copy-start.2 = (bf16[256,128]{1,0:T(8,128)(2,1)S(1)}, bf16[256,128]{1,0:T(8,128)(2,1)}, u32[]{:S(2)}) copy-start(bf16[256,128]{1,0:T(8,128)(2,1)} %get-tuple-element.31.pair_ref) | copy-start | bytes 196612
  85.7 9.7 %copy-start.4 = (bf16[128,128]{1,0:T(8,128)(2,1)S(1)}, bf16[128,128]{1,0:T(8,128)(2,1)}, u32[]{:S(2)}) copy-start(bf16[128,128]{1,0:T(8,128)(2,1)} %cot_ref.3) | copy-start | bytes 98308
  85.7 9.7 %copy-start.6 = (bf16[128,256]{1,0:T(8,128)(2,1)S(1)}, bf16[128,256]{1,0:T(8,128)(2,1)}, u32[]{:S(2)}) copy-start(bf16[128,256]{1,0:T(8,128)(2,1)} %get-tuple-element.34.ae_ref) | copy-start | bytes 196612
  85.7 9.7 %copy-start.8 = (f32[64,128]{1,0:T(8,128)S(1)}, f32[64,128]{1,0:T(8,128)}, u32[]{:S(2)}) copy-start(f32[64,128]{1,0:T(8,128)} %get-tuple-element.35.bw_ref) | copy-start | bytes 98308
  95.5 19.3 %copy-start.1 = (bf16[3072,128]{1,0:T(8,128)(2,1)S(1)}, bf16[3072,128]{1,0:T(8,128)(2,1)}, u32[]{:S(2)}) copy-start(bf16[3072,128]{1,0:T(8,128)(2,1)} %all-gather.1) | copy-start | bytes 2359300
  95.8 7.2 %collective-permute-start = (bf16[704,128]{1,0:T(8,128)(2,1)S(1)}, bf16[704,128]{1,0:T(8,128)(2,1)S(1)}, u32[]{:S(2)}, u32[]{:S(2)}) collective-permute-start(bf16[704,128]{1,0:T(8,128)(2,1)S(1)} %get-tuple-element.37), channel_id=1, source_target_pairs={{0,4},{4,0},{8,12},{12,8},{16,20},{20,16},{24,28},{28,24},{32,36},... | collective-permute-start | bytes 540680 | tf_op jit(solution)/shard_map/ppermute | solution.py:236
  103.1 5.7 %collective-permute-start.1 = (bf16[352,128]{1,0:T(8,128)(2,1)S(1)}, bf16[352,128]{1,0:T(8,128)(2,1)S(1)}, u32[]{:S(2)}, u32[]{:S(2)}) collective-permute-start(bf16[352,128]{1,0:T(8,128)(2,1)S(1)} %get-tuple-element.39), channel_id=1, source_target_pairs={{0,8},{4,12},{8,0},{12,4},{16,24},{20,28},{24,16},{28,20},{32,40},... | collective-permute-start | bytes 270344 | tf_op jit(solution)/shard_map/ppermute | solution.py:236
  108.8 6.0 %copy-start.10 = (s32[128]{0:T(128)S(1)}, s32[128]{0:T(128)}, u32[]{:S(2)}) copy-start(s32[128]{0:T(128)} %param.20) | copy-start | bytes 1540
  108.9 7.4 %collective-permute-start.2 = (bf16[176,128]{1,0:T(8,128)(2,1)S(1)}, bf16[176,128]{1,0:T(8,128)(2,1)S(1)}, u32[]{:S(2)}, u32[]{:S(2)}) collective-permute-start(bf16[176,128]{1,0:T(8,128)(2,1)S(1)} %get-tuple-element.41), channel_id=1, source_target_pairs={{0,16},{4,20},{8,24},{12,28},{16,0},{20,4},{24,8},{28,12},{32,48},... | collective-permute-start | bytes 135176 | tf_op jit(solution)/shard_map/ppermute | solution.py:236
  116.2 0.7 copy-start.9

commit v4 on v3

--- a/solution.py
+++ b/solution.py
@@ -12,21 +12,21 @@
 BF16 = jnp.bfloat16
 VMEM = pl.BlockSpec(memory_space=pltpu.VMEM)
 ROWS = 1408
-STEP = 512
-
-
-def call(kernel, outs, *args, scratch=(), flops=0, limit=20):
+STEP = 2048
+
+
+def call(kernel, outs, *args, scratch=(), flops=0, limit=20, after=()):
     total = sum(math.prod(o.shape) * o.dtype.itemsize for o in outs)
     total += sum(a.size * a.dtype.itemsize for a in args)
     return pl.pallas_call(
         kernel,
         out_shape=list(outs),
-        in_specs=[VMEM] * len(args),
+        in_specs=[VMEM] * len(args) + [pl.BlockSpec(memory_space=pl.ANY)] * len(after),
         out_specs=[VMEM] * len(outs),
         scratch_shapes=list(scratch),
         compiler_params=pltpu.CompilerParams(vmem_limit_bytes=limit * 1024 * 1024),
         cost_estimate=pl.CostEstimate(flops=flops, bytes_accessed=total, transcendentals=0),
-    )(*args)
+    )(*args, *after)
 
 
 def shape(*dims, dtype=F32):
@@ -86,7 +86,7 @@
 def front_kernel(
     all_ref, atom_ref, win_ref, watom_ref, index_ref, send_ref, basis_ref, wb_ref, source_ref,
     target_ref,
-    pre_ref, act_ref, ae_ref, gm_ref, own_ref, both_ref, acc_ref,
+    wide_ref, half_ref, ae_ref, both_ref, acc_ref,
 ):
     at = one_hot(iota(8, 128, 0) == index_ref[...])
     atom_edge = dot_tn(at, atom_ref[...]).astype(BF16)
@@ -97,11 +97,11 @@
     for c in range(4):
         pre = pre + dot(all_ref[c, :128, :], win_ref[c * 128 : (c + 1) * 128, :])
         total = total + dot_nt(all_ref[c, 128:256, :], all_ref[c, mine, :])
-    pre_ref[...] = pre
+    wide_ref[:128, :] = pre
     act = (pre * sigmoid(pre)).astype(BF16)
-    act_ref[...] = act
+    half_ref[:128, :] = act
     gm = total.astype(BF16)
-    gm_ref[...] = gm
+    half_ref[128:, :] = gm
     wb = wb_ref[...]
     rows = acc_ref.shape[0]
     for span, lines in steps(source_ref):
@@ -117,7 +117,7 @@
             acc_ref[...] = part
         else:
             acc_ref[...] += part
-    own_ref[...] = acc_ref[:128, :]
+    wide_ref[128:, :] = acc_ref[:128, :]
     for i in range(8):
         pick = one_hot(iota(128, 128, 0) == send_ref[i : i + 1, :])
         outgoing = dot_tn(pick, act).reshape(16, 8, 128)
@@ -128,25 +128,25 @@
 
 
 def gather_kernel(
-    act_ref, in_ref, own_ref, pre_ref, send_ref, gm_ref, basis_ref, wb_ref, source_ref, target_ref,
+    half_ref, in_ref, wide_ref, send_ref, basis_ref, wb_ref, source_ref, target_ref,
     after_ref,
     pair_ref, bw_ref, ext_ref,
 ):
     got = in_ref[...].astype(F32).reshape(-1, 16, 128)
-    ext_ref[:128, :] = act_ref[...]
+    ext_ref[:128, :] = half_ref[:128, :]
     ext_ref[128:, :] = got[:, :8, :].reshape(-1, 128).astype(BF16)
     back = got[:, 8:, :].reshape(-1, 128).astype(BF16)
-    ga = own_ref[...]
+    ga = wide_ref[128:, :]
     for i in range(8):
         put = one_hot(iota(128, 128, 0) == send_ref[i : i + 1, :])
         ga = ga + dot(put, back[i * 128 : (i + 1) * 128, :])
-    pre = pre_ref[...]
+    pre = wide_ref[:128, :]
     sig = sigmoid(pre)
     pair_ref[128:, :] = (ga * (sig * (1.0 + pre * (1.0 - sig)))).astype(BF16)
     ext = ext_ref[...]
     msg = jnp.zeros((128, 128), F32)
     bw = jnp.zeros(bw_ref.shape, F32)
-    gm = gm_ref[...]
+    gm = half_ref[128:, :]
     wb = wb_ref[...]
     for span, lines in steps(source_ref):
         basis = basis_ref[:, span]
@@ -184,7 +184,7 @@
     out_ref[...] = acc_ref[pl.ds(other, half), :].astype(BF16)
 
 
-def edge_out_kernel(pair_all, weights_ref, index_ref, edge_ref, atom_ref):
+def edge_out_kernel(pair_all, weights_ref, index_ref, edge_ref, atom_ref, done_ref):
     mine = pl.ds(pl.multiple_of(lax.axis_index("col") * 128, 128), 128)
     at = one_hot(iota(8, 128, 0) == index_ref[...])
     edge = jnp.zeros((128, 128), F32)
@@ -198,6 +198,7 @@
         atom = atom + dot_nt(high, weights_ref[c, 512:, :]) + dot_nt(low, weights_ref[c, 512:, :])
     edge_ref[...] = edge.astype(BF16)
     atom_ref[...] = atom
+    done_ref[...] = atom[:, :128]
 
 
 def halve_kernel(level, keep_ref, got_ref, send_ref, own_ref):
@@ -263,11 +264,11 @@
         pack_kernel, [shape(768, 128, **half)], edge_embed, cotangent, weight_out, limit=58
     )
     col_all = lax.all_gather(packed, "col")
-    preact, active, atom_edge, grad_msg, grad_own, both = call(
+    wide, narrow, atom_edge, both = call(
         front_kernel,
         [
-            shape(128, 128), shape(128, 128, **half), shape(128, 256, **half),
-            shape(128, 128, **half), shape(128, 128), shape(2048, 128, **half),
+            shape(256, 128), shape(256, 128, **half), shape(128, 256, **half),
+            shape(2048, 128, **half),
         ],
         col_all, atom_embed, weight_in, weight_atom, index, send, basis, weight_basis, source, target,
         scratch=[pltpu.VMEM((1152, 128), F32)],
@@ -278,16 +279,18 @@
         both.reshape(extent, 16, 128), "space", split_axis=0, concat_axis=0, tiled=True
     ).reshape(2048, 128)
     (weights,) = call(
-        pack_weights_kernel, [shape(768, 128, **half)], weight_in, weight_atom, grad_own
+        pack_weights_kernel, [shape(768, 128, **half)], weight_in, weight_atom,
+        after=(wide,),
     )
     weights = lax.all_gather(weights, "col")
     pair, grad_bw = call(
         gather_kernel,
         [shape(256, 128, **half), shape(64, 128)],
-        active, both, grad_own, preact, send, grad_msg, basis, weight_basis, source, target, weights,
+        narrow, both, wide, send, basis, weight_basis, source, target,
         scratch=[pltpu.VMEM((1152, 128), BF16)],
         flops=2 * 4096 * 1152 * 128,
-        limit=58,
+        limit=50,
+        after=(weights,),
     )
     pair_all = lax.all_gather(pair, "col")
     out, keep = call(
@@ -296,8 +299,10 @@
         col_all, pair_all, pair, atom_edge, cotangent, grad_bw,
         scratch=[pltpu.VMEM((ROWS, 128), F32)],
     )
-    grad_edge, grad_atom = call(
-        edge_out_kernel, [shape(128, 128, **half), shape(8, 256)], pair_all, weights, index
+    grad_edge, grad_atom, done = call(
+        edge_out_kernel,
+        [shape(128, 128, **half), shape(8, 256), shape(8, 128)],
+        pair_all, weights, index,
     )
     rows = ROWS // 2
     for level in (1, 2):
@@ -309,7 +314,8 @@
             keep, got,
         )
     (out,) = call(
-        add_kernel, [shape(rows, 128, **half)], keep, space_swap(out, 4, extent), grad_atom
+        add_kernel, [shape(rows, 128, **half)], keep, space_swap(out, 4, extent),
+        after=(done,),
     )
     depth = extent // 8
     groups = [[z * 8 + g for z in range(depth)] for g in range(8)]

time: 166 us -> 159 us (0.958)
  Pallas kernels: 19.3 us -> 14.2 us
    pallas_call x11, Pallas kernels: 19.3 us -> 14.2 us  [call(): pl.pallas_call(kernel, out_shape=list(outs), in_specs=[VMEM] * len(args)...]
where the time goes in v4:
time: 159 us; the launch traced here: 158 us
  blocking collectives  82.3 us (52%)
  starting transfers between devices  37.7 us (24%)
  waiting for transfers between devices  23.4 us (15%)
  Pallas kernels  14.2 us (9%)
    all_gather x2, blocking collectives, body(): out = lax.all_gather(out, 'space', axis_index_groups=groups)  47.3 us
    all_to_all x1, starting transfers between devices, body(): lax.all_to_all(both.reshape(extent, 16, 128), 'space', split_axis=0, conc...  22.7 us
    all_to_all x1, waiting for transfers between devices, body(): lax.all_to_all(both.reshape(extent, 16, 128), 'space', split_axis=0, conc...  19.3 us
    ppermute x3, starting transfers between devices, space_swap(): lax.ppermute(array, 'space', [(i, i ^ distance) for i in range(extent)])  14.9 us
    pallas_call x11, Pallas kernels, call(): pl.pallas_call(kernel, out_shape=list(outs), in_specs=[VMEM] * len(args)...  14.2 us
    all_gather x1, blocking collectives, body(): col_all = lax.all_gather(packed, 'col')  14 us
    all_gather x1, blocking collectives, body(): weights = lax.all_gather(weights, 'col')  11.4 us
    all_gather x1, blocking collectives, body(): pair_all = lax.all_gather(pair, 'col')  9.5 us
  transfers between devices with their start and end apart: 4, of which 4 were waited for; matrix products, arithmetic and copies ran while one was open for 0% of the time, Pallas kernels for 1%

profile of v4, /device:TPU:1, one launch (start us, length us, event | category | flops | bytes accessed | tf_op | source)
XLA Modules:
  0.0 158.5 jit_solution(3992511410947375140)
XLA Ops:
  0.6 1.6 %shard_map.163 = bf16[768,128]{1,0:T(8,128)(2,1)} custom-call(bf16[128,128]{1,0:T(8,128)(2,1)} %edge_ref.1, bf16[128,128]{1,0:T(8,128)(2,1)} %cot_ref.3, bf16[512,128]{1,0:T(8,128)(2,1)} %wout_ref.1), custom_call_target="tpu_custom_call" | custom-call | bytes 393216 | tf_op jit(solution)/shard_map/pallas_call | solution.py:21
  2.3 14.0 %all-gather = bf16[3072,128]{1,0:T(8,128)(2,1)} all-gather(bf16[768,128]{1,0:T(8,128)(2,1)} %shard_map.163), channel_id=2, replica_groups=mesh['space'=128,'col'=4] {'col'}, dimensions={0}, use_global_device_ids=true | all-gather | bytes 983040 | tf_op jit(solution)/shard_map/all_gather | solution.py:266
  16.3 5.9 %shard_map.164 = (f32[256,128]{1,0:T(8,128)}, bf16[256,128]{1,0:T(8,128)(2,1)}, bf16[128,256]{1,0:T(8,128)(2,1)}, bf16[2048,128]{1,0:T(8,128)(2,1)}) custom-call(bf16[4,768,128]{2,1,0:T(8,128)(2,1)} %bitcast.12, bf16[8,256]{1,0:T(8,128)(2,1)} %atom_ref.1, bf16[512,128]{1,0:T(8,128)(2,1)} %win_ref.3, bf16[256,128]{1,0:T(8,128)(2,1)} %watom_ref.3, ...), custom_call_target="tpu_custom_call" | custom-call | flops 1207959552 | bytes 2351616 | tf_op jit(solution)/shard_map/pallas_call | solution.py:21
  22.2 0.0 copy-start.5
  22.2 22.7 %all-to-all-start = ((bf16[128,16,128]{2,1,0:T(8,128)(2,1)}), bf16[128,16,128]{2,1,0:T(8,128)(2,1)S(1)}, u32[]{:S(2)}, u32[]{:S(2)}) async-start(bf16[128,16,128]{2,1,0:T(8,128)(2,1)} %bitcast.31), calls=%async_computation | async-start | bytes 1048576 | tf_op jit(solution)/shard_map/all_to_all | solution.py:278
  45.0 0.0 copy-start.7
  45.0 0.0 copy-start.8
  45.0 0.0 copy-start.9
  45.1 0.0 copy-start.10
  45.1 0.0 copy-start.12
  45.1 11.4 %all-gather.1 = bf16[3072,128]{1,0:T(8,128)(2,1)S(1)} all-gather(bf16[768,128]{1,0:T(8,128)(2,1)S(1)} %shard_map.165), channel_id=3, replica_groups=mesh['space'=128,'col'=4] {'col'}, dimensions={0}, use_global_device_ids=true | all-gather | bytes 983040 | tf_op jit(solution)/shard_map/all_gather | solution.py:285
  56.5 19.3 %all-to-all-done = bf16[128,16,128]{2,1,0:T(8,128)(2,1)S(1)} async-done(((bf16[128,16,128]{2,1,0:T(8,128)(2,1)}), bf16[128,16,128]{2,1,0:T(8,128)(2,1)S(1)}, u32[]{:S(2)}, u32[]{:S(2)}) %all-to-all-start) | async-done | bytes 524320 | tf_op jit(solution)/shard_map/all_to_all | solution.py:278
  75.8 0.0 copy-done.8
  75.8 4.0 %shard_map.166 = (bf16[256,128]{1,0:T(8,128)(2,1)S(1)}, f32[64,128]{1,0:T(8,128)S(1)}) custom-call(bf16[256,128]{1,0:T(8,128)(2,1)S(1)} %copy-done.12, bf16[2048,128]{1,0:T(8,128)(2,1)S(1)} %bitcast.20, f32[256,128]{1,0:T(8,128)S(1)} %copy-done.3, s32[8,128]{1,0:T(8,128)S(1)} %bitcast.30, bf16[64,4096]{1,0:T(8,128)(2,1)S(1)} %bitcast.24, ...), custom_call_target="tpu_custom_call" | custom-call | flops 1207959552 | bytes 1396736 | tf_op jit(solution)/shard_map/pallas_call | solution.py:21
  79.8 0.0 copy-start.1
  79.9 0.0 copy-start.4
  79.9 9.5 %all-gather.2 = bf16[1024,128]{1,0:T(8,128)(2,1)S(1)} all-gather(bf16[256,128]{1,0:T(8,128)(2,1)S(1)} %get-tuple-element.28.pair_ref), channel_id=4, replica_groups=mesh['space'=128,'col'=4] {'col'}, dimensions={0}, use_global_device_ids=true | all-gather | bytes 327680 | tf_op jit(solution)/shard_map/all_gather | solution.py:295
  89.4 0.0 copy-done
  89.4 0.0 copy-done.4
  89.4 0.4 shard_map.168
  89.8 6.2 %collective-permute-start = (bf16[704,128]{1,0:T(8,128)(2,1)S(1)}, bf16[704,128]{1,0:T(8,128)(2,1)S(1)}, u32[]{:S(2)}, u32[]{:S(2)}) collective-permute-start(bf16[704,128]{1,0:T(8,128)(2,1)S(1)} %get-tuple-element.34), channel_id=1, source_target_pairs={{0,4},{4,0},{8,12},{12,8},{16,20},{20,16},{24,28},{28,24},{32,36},... | collective-permute-start | bytes 540680 | tf_op jit(solution)/shard_map/ppermute | solution.py:237
  96.0 1.0 collective-permute-done.got_ref
  97.0 2.8 %collective-permute-start.1 = (bf16[352,128]{1,0:T(8,128)(2,1)S(1)}, bf16[352,128]{1,0:T(8,128)(2,1)S(1)}, u32[]{:S(2)}, u32[]{:S(2)}) collective-permute-start(bf16[352,128]{1,0:T(8,128)(2,1)S(1)} %get-tuple-element.36), channel_id=1, source_target_pairs={{0,8},{4,12},{8,0},{12,4},{16,24},{20,28},{24,16},{28,20},{32,40},... | collective-permute-start | bytes 270344 | tf_op jit(solution)/shard_map/ppermute | solution.py:237
  99.8 2.9 %collective-permute-done.1.got_ref = bf16[352,128]{1,0:T(8,128)(2,1)S(1)} collective-permute-done((bf16[352,128]{1,0:T(8,128)(2,1)S(1)}, bf16[352,128]{1,0:T(8,128)(2,1)S(1)}, u32[]{:S(2)}, u32[]{:S(2)}) %collective-permute-start.1) | collective-permute-done | bytes 90144 | tf_op jit(solution)/shard_map/ppermute | solution.py:237
  102.8 0.0 copy-start.6
  102.8 5.9 %collective-permute-start.2 = (bf16[176,128]{1,0:T(8,128)(2,1)S(1)}, bf16[176,128]{1,0:T(8,128)(2,1)S(1)}, u32[]{:S(2)}, u32[]{:S(2)}) collective-permute-start(bf16[176,128]{1,0:T(8,128)(2,1)S(1)} %get-tuple-element.38), channel_id=1, source_target_pairs={{0,16},{4,20},{8,24},{12,28},{16,0},{20,4},{24,8},{28,12},{32,48},... | collective-permute-start | bytes 135176 | tf_op jit(solution)/shard_map/ppermute | solution.py:237
  108.7 1.2 shard_map.167
  110.0 0.2 collective-permute-done.2.got_ref
  110.2 25.1 %all-gather.3 = bf16[2816,128]{1,0:T(8,128)(2,1)S(1)} all-gather(bf16[176,128]{1,0:T(8,128)(2,1)S(1)} %shard_map.171), channel_id=5, replica_groups={{0,32,64,96,128,160,192,224,256,288,320,352,384,416,448,480},{4,36,68,1..., dimensions={0}, use_global_device_ids=true | all-gather | bytes 765952 | tf_op jit(solution)/shard_map/all_gather | solution.py:322
  135.3 0.1 shard_map.172
  135.4 22.2 %all-gather.4 = bf16[1408,128]{1,0:T(8,128)(2,1)S(1)} all-gather(bf16[176,128]{1,0:T(8,128)(2,1)S(1)} %shard_map.172), channel_id=6, replica_groups={{0,4,8,12,16,20,24,28},{32,36,40,44,48,52,56,60},{64,68,72,76,80,84,88,..., dimensions={0}, use_global_device_ids=true | all-gather | bytes 405504 | tf_op jit(solution)/shard_map/all_gather | solution.py:325
  157.6 0.9 shard_map.173
  (18 shorter events, 0.1 us)
Async XLA Ops:
  22.2 22.8 %copy-start.2 = (bf16[512,128]{1,0:T(8,128)(2,1)S(1)}, bf16[512,128]{1,0:T(8,128)(2,1)}, u32[]{:S(2)}) copy-start(bf16[512,128]{1,0:T(8,128)(2,1)} %win_ref.3) | copy-start | bytes 393220
  22.2 22.8 %copy-start.3 = (f32[256,128]{1,0:T(8,128)S(1)}, f32[256,128]{1,0:T(8,128)}, u32[]{:S(2)}) copy-start(f32[256,128]{1,0:T(8,128)} %get-tuple-element.27.after_ref.wide_ref) | copy-start | bytes 393220
  22.2 22.8 %copy-start.5 = (bf16[256,128]{1,0:T(8,128)(2,1)S(1)}, bf16[256,128]{1,0:T(8,128)(2,1)}, u32[]{:S(2)}) copy-start(bf16[256,128]{1,0:T(8,128)(2,1)} %watom_ref.3) | copy-start | bytes 196612
  22.2 53.6 %all-to-all-start = ((bf16[128,16,128]{2,1,0:T(8,128)(2,1)}), bf16[128,16,128]{2,1,0:T(8,128)(2,1)S(1)}, u32[]{:S(2)}, u32[]{:S(2)}) async-start(bf16[128,16,128]{2,1,0:T(8,128)(2,1)} %bitcast.31), calls=%async_computation | async-start | bytes 1048576 | tf_op jit(solution)/shard_map/all_to_all | solution.py:278
  45.0 30.8 %copy-start.7 = (bf16[4096,64]{0,1:T(8,128)(2,1)S(1)}, bf16[4096,64]{0,1:T(8,128)(2,1)}, u32[]{:S(2)}) copy-start(bf16[4096,64]{0,1:T(8,128)(2,1)} %param.15) | copy-start | bytes 1572868
  45.0 30.8 %copy-start.8 = (bf16[64,128]{1,0:T(8,128)(2,1)S(1)}, bf16[64,128]{1,0:T(8,128)(2,1)}, u32[]{:S(2)}) copy-start(bf16[64,128]{1,0:T(8,128)(2,1)} %wb_ref.3) | copy-start | bytes 49156
  45.0 30.8 %copy-start.9 = (s32[4096]{0:T(1024)S(1)}, s32[4096]{0:T(1024)}, u32[]{:S(2)}) copy-start(s32[4096]{0:T(1024)} %param.21) | copy-start | bytes 49156
  45.1 30.7 %copy-start.10 = (s32[4096]{0:T(1024)S(1)}, s32[4096]{0:T(1024)}, u32[]{:S(2)}) copy-start(s32[4096]{0:T(1024)} %param.22) | copy-start | bytes 49156
  45.1 30.7 %copy-start.12 = (bf16[256,128]{1,0:T(8,128)(2,1)S(1)}, bf16[256,128]{1,0:T(8,128)(2,1)}, u32[]{:S(2)}) copy-start(bf16[256,128]{1,0:T(8,128)(2,1)} %get-tuple-element.25.half_ref) | copy-start | bytes 196612
  56.5 19.3 %copy-start.11 = (s32[1,1024]{1,0:T(1,128)S(1)}, s32[1,1024]{1,0:T(1,128)}, u32[]{:S(2)}) copy-start(s32[1,1024]{1,0:T(1,128)} %param.23) | copy-start | bytes 12292
  75.8 13.6 %copy-start = (bf16[3072,128]{1,0:T(8,128)(2,1)S(1)}, bf16[3072,128]{1,0:T(8,128)(2,1)}, u32[]{:S(2)}) copy-start(bf16[3072,128]{1,0:T(8,128)(2,1)} %all-gather) | copy-start | bytes 2359300
  79.8 9.5 %copy-start.1 = (bf16[128,128]{1,0:T(8,128)(2,1)S(1)}, bf16[128,128]{1,0:T(8,128)(2,1)}, u32[]{:S(2)}) copy-start(bf16[128,128]{1,0:T(8,128)(2,1)} %cot_ref.3) | copy-start | bytes 98308
  79.9 9.5 %copy-start.4 = (bf16[128,256]{1,0:T(8,128)(2,1)S(1)}, bf16[128,256]{1,0:T(8,128)(2,1)}, u32[]{:S(2)}) copy-start(bf16[128,256]{1,0:T(8,128)(2,1)} %get-tuple-element.31.ae_ref) | copy-start | bytes 196612
  89.8 7.2 %collective-permute-start = (bf16[704,128]{1,0:T(8,128)(2,1)S(1)}, bf16[704,128]{1,0:T(8,128)(2,1)S(1)}, u32[]{:S(2)}, u32[]{:S(2)}) collective-permute-start(bf16[704,128]{1,0:T(8,128)(2,1)S(1)} %get-tuple-element.34), channel_id=1, source_target_pairs={{0,4},{4,0},{8,12},{12,8},{16,20},{20,16},{24,28},{28,24},{32,36},... | collective-permute-start | bytes 540680 | tf_op jit(solution)/shard_map/ppermute | solution.py:237
  97.0 5.7 %collective-permute-start.1 = (bf16[352,128]{1,0:T(8,128)(2,1)S(1)}, bf16[352,128]{1,0:T(8,128)(2,1)S(1)}, u32[]{:S(2)}, u32[]{:S(2)}) collective-permute-start(bf16[352,128]{1,0:T(8,128)(2,1)S(1)} %get-tuple-element.36), channel_id=1, source_target_pairs={{0,8},{4,12},{8,0},{12,4},{16,24},{20,28},{24,16},{28,20},{32,40},... | collective-permute-start | bytes 270344 | tf_op jit(solution)/shard_map/ppermute | solution.py:237
  102.8 6.0 %copy-start.6 = (s32[128]{0:T(128)S(1)}, s32[128]{0:T(128)}, u32[]{:S(2)}) copy-start(s32[128]{0:T(128)} %param.20) | copy-start | bytes 1540
  102.8 7.4 %collective-permute-start.2 = (bf16[176,128]{1,0:T(8,128)(2,1)S(1)}, bf16[176,128]{1,0:T(8,128)(2,1)S(1)}, u32[]{:S(2)}, u32[]{:S(2)}) collective-permute-start(bf16[176,128]{1,0:T(8,128)(2,1)S(1)} %get-tuple-element.38), channel_id=1, source_target_pairs={{0,16},{4,20},{8,24},{12,28},{16,0},{20,4},{24,8},{28,12},{32,48},... | collective-permute-start | bytes 135176 | tf_op jit(solution)/shard_map/ppermute | solution.py:237

commit v5 on v4

--- a/solution.py
+++ b/solution.py
@@ -12,7 +12,7 @@
 BF16 = jnp.bfloat16
 VMEM = pl.BlockSpec(memory_space=pltpu.VMEM)
 ROWS = 1408
-STEP = 2048
+STEP = 4096
 
 
 def call(kernel, outs, *args, scratch=(), flops=0, limit=20, after=()):
@@ -201,7 +201,8 @@
     done_ref[...] = atom[:, :128]
 
 
-def halve_kernel(level, keep_ref, got_ref, send_ref, own_ref):
+def halve_kernel(level, keep_ref, got_ref, *refs):
+    send_ref, own_ref = refs[-2:]
     half = send_ref.shape[0]
     mine = pl.multiple_of(bit_of(level) * half, 16)
     other = pl.multiple_of(half - mine, 16)
@@ -211,7 +212,7 @@
     own_ref[...] = keep_ref[pl.ds(mine, half), :] + got_ref[pl.ds(mine, half), :].astype(F32)
 
 
-def add_kernel(own_ref, got_ref, after_ref, out_ref):
+def add_kernel(own_ref, got_ref, out_ref):
     out_ref[...] = (own_ref[...] + got_ref[...].astype(F32)).astype(BF16)
 
 
@@ -312,10 +313,10 @@
             functools.partial(halve_kernel, level),
             [shape(rows, 128, **half), shape(rows, 128)],
             keep, got,
+            after=(done,) if level == 2 else (),
         )
     (out,) = call(
-        add_kernel, [shape(rows, 128, **half)], keep, space_swap(out, 4, extent),
-        after=(done,),
+        add_kernel, [shape(rows, 128, **half)], keep, space_swap(out, 4, extent)
     )
     depth = extent // 8
     groups = [[z * 8 + g for z in range(depth)] for g in range(8)]

time: 159 us -> 160 us (level)
  no operation moved by 1% of the time
where the time goes in v5:
time: 160 us
  blocking collectives  82.3 us (51%)
  starting transfers between devices  37.7 us (24%)
  waiting for transfers between devices  23.4 us (15%)
  Pallas kernels  15.7 us (10%)
    all_gather x2, blocking collectives, body(): out = lax.all_gather(out, 'space', axis_index_groups=groups)  47.3 us
    all_to_all x1, starting transfers between devices, body(): lax.all_to_all(both.reshape(extent, 16, 128), 'space', split_axis=0, conc...  22.7 us
    all_to_all x1, waiting for transfers between devices, body(): lax.all_to_all(both.reshape(extent, 16, 128), 'space', split_axis=0, conc...  19.3 us
    pallas_call x11, Pallas kernels, call(): pl.pallas_call(kernel, out_shape=list(outs), in_specs=[VMEM] * len(args)...  15.7 us
    ppermute x3, starting transfers between devices, space_swap(): lax.ppermute(array, 'space', [(i, i ^ distance) for i in range(extent)])  14.9 us
    all_gather x1, blocking collectives, body(): col_all = lax.all_gather(packed, 'col')  14 us
    all_gather x1, blocking collectives, body(): weights = lax.all_gather(weights, 'col')  11.4 us
    all_gather x1, blocking collectives, body(): pair_all = lax.all_gather(pair, 'col')  9.5 us
  transfers between devices with their start and end apart: 4, of which 4 were waited for; matrix products, arithmetic and copies ran while one was open for 0% of the time, Pallas kernels for 1%

profile of v5, /device:TPU:1, one launch (start us, length us, event | category | flops | bytes accessed | tf_op | source)
XLA Modules:
  0.0 160.0 jit_solution(6742059880473957114)
XLA Ops:
  0.6 1.6 %shard_map.163 = bf16[768,128]{1,0:T(8,128)(2,1)} custom-call(bf16[128,128]{1,0:T(8,128)(2,1)} %edge_ref.1, bf16[128,128]{1,0:T(8,128)(2,1)} %cot_ref.3, bf16[512,128]{1,0:T(8,128)(2,1)} %wout_ref.1), custom_call_target="tpu_custom_call" | custom-call | bytes 393216 | tf_op jit(solution)/shard_map/pallas_call | solution.py:21
  2.3 14.0 %all-gather = bf16[3072,128]{1,0:T(8,128)(2,1)} all-gather(bf16[768,128]{1,0:T(8,128)(2,1)} %shard_map.163), channel_id=2, replica_groups=mesh['space'=128,'col'=4] {'col'}, dimensions={0}, use_global_device_ids=true | all-gather | bytes 983040 | tf_op jit(solution)/shard_map/all_gather | solution.py:267
  16.3 6.7 %shard_map.164 = (f32[256,128]{1,0:T(8,128)}, bf16[256,128]{1,0:T(8,128)(2,1)}, bf16[128,256]{1,0:T(8,128)(2,1)}, bf16[2048,128]{1,0:T(8,128)(2,1)}) custom-call(bf16[4,768,128]{2,1,0:T(8,128)(2,1)} %bitcast.12, bf16[8,256]{1,0:T(8,128)(2,1)} %atom_ref.1, bf16[512,128]{1,0:T(8,128)(2,1)} %win_ref.3, bf16[256,128]{1,0:T(8,128)(2,1)} %watom_ref.3, ...), custom_call_target="tpu_custom_call" | custom-call | flops 1207959552 | bytes 2351616 | tf_op jit(solution)/shard_map/pallas_call | solution.py:21
  22.9 0.0 copy-start.5
  23.0 22.7 %all-to-all-start = ((bf16[128,16,128]{2,1,0:T(8,128)(2,1)}), bf16[128,16,128]{2,1,0:T(8,128)(2,1)S(1)}, u32[]{:S(2)}, u32[]{:S(2)}) async-start(bf16[128,16,128]{2,1,0:T(8,128)(2,1)} %bitcast.31), calls=%async_computation | async-start | bytes 1048576 | tf_op jit(solution)/shard_map/all_to_all | solution.py:279
  45.8 0.0 copy-start.7
  45.8 0.0 copy-start.8
  45.8 0.0 copy-start.9
  45.8 0.0 copy-start.10
  45.8 0.0 copy-start.12
  45.8 11.4 %all-gather.1 = bf16[3072,128]{1,0:T(8,128)(2,1)S(1)} all-gather(bf16[768,128]{1,0:T(8,128)(2,1)S(1)} %shard_map.165), channel_id=3, replica_groups=mesh['space'=128,'col'=4] {'col'}, dimensions={0}, use_global_device_ids=true | all-gather | bytes 983040 | tf_op jit(solution)/shard_map/all_gather | solution.py:286
  57.3 19.3 %all-to-all-done = bf16[128,16,128]{2,1,0:T(8,128)(2,1)S(1)} async-done(((bf16[128,16,128]{2,1,0:T(8,128)(2,1)}), bf16[128,16,128]{2,1,0:T(8,128)(2,1)S(1)}, u32[]{:S(2)}, u32[]{:S(2)}) %all-to-all-start) | async-done | bytes 524320 | tf_op jit(solution)/shard_map/all_to_all | solution.py:279
  76.5 0.0 copy-done.8
  76.6 4.7 %shard_map.166 = (bf16[256,128]{1,0:T(8,128)(2,1)S(1)}, f32[64,128]{1,0:T(8,128)S(1)}) custom-call(bf16[256,128]{1,0:T(8,128)(2,1)S(1)} %copy-done.12, bf16[2048,128]{1,0:T(8,128)(2,1)S(1)} %bitcast.20, f32[256,128]{1,0:T(8,128)S(1)} %copy-done.3, s32[8,128]{1,0:T(8,128)S(1)} %bitcast.30, bf16[64,4096]{1,0:T(8,128)(2,1)S(1)} %bitcast.24, ...), custom_call_target="tpu_custom_call" | custom-call | flops 1207959552 | bytes 1396736 | tf_op jit(solution)/shard_map/pallas_call | solution.py:21
  81.3 0.0 copy-start.1
  81.3 0.0 copy-start.4
  81.4 9.5 %all-gather.2 = bf16[1024,128]{1,0:T(8,128)(2,1)S(1)} all-gather(bf16[256,128]{1,0:T(8,128)(2,1)S(1)} %get-tuple-element.28.pair_ref), channel_id=4, replica_groups=mesh['space'=128,'col'=4] {'col'}, dimensions={0}, use_global_device_ids=true | all-gather | bytes 327680 | tf_op jit(solution)/shard_map/all_gather | solution.py:296
  90.9 0.0 copy-done
  90.9 0.0 copy-done.4
  90.9 0.4 shard_map.168
  91.2 6.2 %collective-permute-start = (bf16[704,128]{1,0:T(8,128)(2,1)S(1)}, bf16[704,128]{1,0:T(8,128)(2,1)S(1)}, u32[]{:S(2)}, u32[]{:S(2)}) collective-permute-start(bf16[704,128]{1,0:T(8,128)(2,1)S(1)} %get-tuple-element.34), channel_id=1, source_target_pairs={{0,4},{4,0},{8,12},{12,8},{16,20},{20,16},{24,28},{28,24},{32,36},... | collective-permute-start | bytes 540680 | tf_op jit(solution)/shard_map/ppermute | solution.py:238
  97.5 1.0 collective-permute-done.got_ref
  98.5 0.0 copy-start.6
  98.5 2.8 %collective-permute-start.1 = (bf16[352,128]{1,0:T(8,128)(2,1)S(1)}, bf16[352,128]{1,0:T(8,128)(2,1)S(1)}, u32[]{:S(2)}, u32[]{:S(2)}) collective-permute-start(bf16[352,128]{1,0:T(8,128)(2,1)S(1)} %get-tuple-element.36), channel_id=1, source_target_pairs={{0,8},{4,12},{8,0},{12,4},{16,24},{20,28},{24,16},{28,20},{32,40},... | collective-permute-start | bytes 270344 | tf_op jit(solution)/shard_map/ppermute | solution.py:238
  101.3 1.2 shard_map.167
  102.6 1.7 %collective-permute-done.1.got_ref = bf16[352,128]{1,0:T(8,128)(2,1)S(1)} collective-permute-done((bf16[352,128]{1,0:T(8,128)(2,1)S(1)}, bf16[352,128]{1,0:T(8,128)(2,1)S(1)}, u32[]{:S(2)}, u32[]{:S(2)}) %collective-permute-start.1) | collective-permute-done | bytes 90144 | tf_op jit(solution)/shard_map/ppermute | solution.py:238
  104.3 5.9 %collective-permute-start.2 = (bf16[176,128]{1,0:T(8,128)(2,1)S(1)}, bf16[176,128]{1,0:T(8,128)(2,1)S(1)}, u32[]{:S(2)}, u32[]{:S(2)}) collective-permute-start(bf16[176,128]{1,0:T(8,128)(2,1)S(1)} %get-tuple-element.39), channel_id=1, source_target_pairs={{0,16},{4,20},{8,24},{12,28},{16,0},{20,4},{24,8},{28,12},{32,48},... | collective-permute-start | bytes 135176 | tf_op jit(solution)/shard_map/ppermute | solution.py:238
  110.2 1.4 collective-permute-done.2.got_ref
  111.7 25.1 %all-gather.3 = bf16[2816,128]{1,0:T(8,128)(2,1)S(1)} all-gather(bf16[176,128]{1,0:T(8,128)(2,1)S(1)} %shard_map.171), channel_id=5, replica_groups={{0,32,64,96,128,160,192,224,256,288,320,352,384,416,448,480},{4,36,68,1..., dimensions={0}, use_global_device_ids=true | all-gather | bytes 765952 | tf_op jit(solution)/shard_map/all_gather | solution.py:323
  136.8 0.1 shard_map.172
  136.9 22.2 %all-gather.4 = bf16[1408,128]{1,0:T(8,128)(2,1)S(1)} all-gather(bf16[176,128]{1,0:T(8,128)(2,1)S(1)} %shard_map.172), channel_id=6, replica_groups={{0,4,8,12,16,20,24,28},{32,36,40,44,48,52,56,60},{64,68,72,76,80,84,88,..., dimensions={0}, use_global_device_ids=true | all-gather | bytes 405504 | tf_op jit(solution)/shard_map/all_gather | solution.py:326
  159.1 0.9 shard_map.173
  (18 shorter events, 0.1 us)
Async XLA Ops:
  22.9 22.8 %copy-start.2 = (bf16[512,128]{1,0:T(8,128)(2,1)S(1)}, bf16[512,128]{1,0:T(8,128)(2,1)}, u32[]{:S(2)}) copy-start(bf16[512,128]{1,0:T(8,128)(2,1)} %win_ref.3) | copy-start | bytes 393220
  22.9 22.8 %copy-start.3 = (f32[256,128]{1,0:T(8,128)S(1)}, f32[256,128]{1,0:T(8,128)}, u32[]{:S(2)}) copy-start(f32[256,128]{1,0:T(8,128)} %get-tuple-element.27.after_ref.wide_ref) | copy-start | bytes 393220
  22.9 22.8 %copy-start.5 = (bf16[256,128]{1,0:T(8,128)(2,1)S(1)}, bf16[256,128]{1,0:T(8,128)(2,1)}, u32[]{:S(2)}) copy-start(bf16[256,128]{1,0:T(8,128)(2,1)} %watom_ref.3) | copy-start | bytes 196612
  23.0 53.6 %all-to-all-start = ((bf16[128,16,128]{2,1,0:T(8,128)(2,1)}), bf16[128,16,128]{2,1,0:T(8,128)(2,1)S(1)}, u32[]{:S(2)}, u32[]{:S(2)}) async-start(bf16[128,16,128]{2,1,0:T(8,128)(2,1)} %bitcast.31), calls=%async_computation | async-start | bytes 1048576 | tf_op jit(solution)/shard_map/all_to_all | solution.py:279
  45.8 30.8 %copy-start.7 = (bf16[4096,64]{0,1:T(8,128)(2,1)S(1)}, bf16[4096,64]{0,1:T(8,128)(2,1)}, u32[]{:S(2)}) copy-start(bf16[4096,64]{0,1:T(8,128)(2,1)} %param.15) | copy-start | bytes 1572868
  45.8 30.8 %copy-start.8 = (bf16[64,128]{1,0:T(8,128)(2,1)S(1)}, bf16[64,128]{1,0:T(8,128)(2,1)}, u32[]{:S(2)}) copy-start(bf16[64,128]{1,0:T(8,128)(2,1)} %wb_ref.3) | copy-start | bytes 49156
  45.8 30.8 %copy-start.9 = (s32[4096]{0:T(1024)S(1)}, s32[4096]{0:T(1024)}, u32[]{:S(2)}) copy-start(s32[4096]{0:T(1024)} %param.21) | copy-start | bytes 49156
  45.8 30.7 %copy-start.10 = (s32[4096]{0:T(1024)S(1)}, s32[4096]{0:T(1024)}, u32[]{:S(2)}) copy-start(s32[4096]{0:T(1024)} %param.22) | copy-start | bytes 49156
  45.8 30.7 %copy-start.12 = (bf16[256,128]{1,0:T(8,128)(2,1)S(1)}, bf16[256,128]{1,0:T(8,128)(2,1)}, u32[]{:S(2)}) copy-start(bf16[256,128]{1,0:T(8,128)(2,1)} %get-tuple-element.25.half_ref) | copy-start | bytes 196612
  57.3 19.3 %copy-start.11 = (s32[1,1024]{1,0:T(1,128)S(1)}, s32[1,1024]{1,0:T(1,128)}, u32[]{:S(2)}) copy-start(s32[1,1024]{1,0:T(1,128)} %param.23) | copy-start | bytes 12292
  76.6 14.3 %copy-start = (bf16[3072,128]{1,0:T(8,128)(2,1)S(1)}, bf16[3072,128]{1,0:T(8,128)(2,1)}, u32[]{:S(2)}) copy-start(bf16[3072,128]{1,0:T(8,128)(2,1)} %all-gather) | copy-start | bytes 2359300
  81.3 9.5 %copy-start.1 = (bf16[128,128]{1,0:T(8,128)(2,1)S(1)}, bf16[128,128]{1,0:T(8,128)(2,1)}, u32[]{:S(2)}) copy-start(bf16[128,128]{1,0:T(8,128)(2,1)} %cot_ref.3) | copy-start | bytes 98308
  81.3 9.5 %copy-start.4 = (bf16[128,256]{1,0:T(8,128)(2,1)S(1)}, bf16[128,256]{1,0:T(8,128)(2,1)}, u32[]{:S(2)}) copy-start(bf16[128,256]{1,0:T(8,128)(2,1)} %get-tuple-element.31.ae_ref) | copy-start | bytes 196612
  91.2 7.2 %collective-permute-start = (bf16[704,128]{1,0:T(8,128)(2,1)S(1)}, bf16[704,128]{1,0:T(8,128)(2,1)S(1)}, u32[]{:S(2)}, u32[]{:S(2)}) collective-permute-start(bf16[704,128]{1,0:T(8,128)(2,1)S(1)} %get-tuple-element.34), channel_id=1, source_target_pairs={{0,4},{4,0},{8,12},{12,8},{16,20},{20,16},{24,28},{28,24},{32,36},... | collective-permute-start | bytes 540680 | tf_op jit(solution)/shard_map/ppermute | solution.py:238
  98.5 2.8 %copy-start.6 = (s32[128]{0:T(128)S(1)}, s32[128]{0:T(128)}, u32[]{:S(2)}) copy-start(s32[128]{0:T(128)} %param.20) | copy-start | bytes 1540
  98.5 5.7 %collective-permute-start.1 = (bf16[352,128]{1,0:T(8,128)(2,1)S(1)}, bf16[352,128]{1,0:T(8,128)(2,1)S(1)}, u32[]{:S(2)}, u32[]{:S(2)}) collective-permute-start(bf16[352,128]{1,0:T(8,128)(2,1)S(1)} %get-tuple-element.36), channel_id=1, source_target_pairs={{0,8},{4,12},{8,0},{12,4},{16,24},{20,28},{24,16},{28,20},{32,40},... | collective-permute-start | bytes 270344 | tf_op jit(solution)/shard_map/ppermute | solution.py:238
  104.3 7.4 %collective-permute-start.2 = (bf16[176,128]{1,0:T(8,128)(2,1)S(1)}, bf16[176,128]{1,0:T(8,128)(2,1)S(1)}, u32[]{:S(2)}, u32[]{:S(2)}) collective-permute-start(bf16[176,128]{1,0:T(8,128)(2,1)S(1)} %get-tuple-element.39), channel_id=1, source_target_pairs={{0,16},{4,20},{8,24},{12,28},{16,0},{20,4},{24,8},{28,12},{32,48},... | collective-permute-start | bytes 135176 | tf_op jit(solution)/shard_map/ppermute | solution.py:238
